TPU v7x, 32 devices: a whole 2x2x4 slice. The times are simulated.
32 devices in a mesh: pipe: 4 (over y, core), tp: 8 (over z, x).
Axes of the slice: x: 2, y: 2, z: 4, core: 2. Of those that a mesh axis runs over, the one named last changes fastest.
Arguments:
- grad_next: bfloat16 [4, 2048, 8192], P('pipe', None, 'tp'), may hold values from -6 to 6
- inputs: bfloat16 [4, 2048, 8192], P('pipe', None, 'tp'), may hold values from -6 to 6
- dt_raw: bfloat16 [4, 2048, 128], P('pipe', None, 'tp'), may hold values from -5 to 5
- b_proj: bfloat16 [4, 2048, 1024], P('pipe', None, 'tp'), may hold values from -0.375 to 0.375
- c_proj: bfloat16 [4, 2048, 1024], P('pipe', None, 'tp'), may hold values from -0.375 to 0.375
- a_log: float32 [4, 128], P('pipe', 'tp'), may hold values from -7 to -3
- dt_bias: float32 [4, 128], P('pipe', 'tp'), may hold values from -2 to 0.5
- skip_gain: float32 [4, 128], P('pipe', 'tp'), may hold values from 0.5 to 1.5
Outputs:
- grad_inputs: bfloat16 [4, 2048, 8192], P('pipe', None, 'tp')
- grad_dt: bfloat16 [4, 2048, 128], P('pipe', None, 'tp')
All inputs are finite; a program needn't handle non-finite values.
Results may differ from a plain program's by a relative error of at most 0.001.
Values may be sent and summed in bfloat16 or wider, within the bound.
A program may use at most 192 MiB of HBM per device.

v0:
```python
import jax
import jax.numpy as jnp
from jax import lax
from jax.sharding import PartitionSpec as P

P_SIZE = 64
N = 256
G = 4
SPAN = 256


def shifted(value, axis, by):
    length = lax.axis_size(axis)
    return lax.ppermute(value, axis, [(i, (i + by) % length) for i in range(length)])


def ssd_group(values, dt_in, a_log, bias, skip, b_rows, c_rows):
    highest = lax.Precision.HIGHEST
    length, head_count, head_width = values.shape
    block_count = length // SPAN
    step_size = jax.nn.softplus(dt_in + bias[None, :])
    log_decay = (-jnp.exp(a_log)[None, :] * step_size).reshape(block_count, SPAN, head_count)
    cumulative = jnp.cumsum(log_decay, axis=1)
    scaled_x = (values * step_size[:, :, None]).reshape(block_count, SPAN, head_count, head_width)
    b_blocks = b_rows.reshape(block_count, SPAN, b_rows.shape[1])
    c_blocks = c_rows.reshape(block_count, SPAN, c_rows.shape[1])
    scores = jnp.einsum("kin,kjn->kij", c_blocks, b_blocks, precision=highest)
    spread = cumulative[:, :, None, :] - cumulative[:, None, :, :]
    causal = (jnp.arange(SPAN)[:, None] >= jnp.arange(SPAN)[None, :])[None, :, :, None]
    within = jnp.exp(jnp.where(causal, spread, -1e30))
    weights = scores[:, :, :, None] * within
    inner = jnp.einsum("kijh,kjhp->kihp", weights, scaled_x, precision=highest)
    to_end = jnp.exp(cumulative[:, -1:, :] - cumulative)
    states = jnp.einsum(
        "kjhp,kjn->khpn", scaled_x * to_end[:, :, :, None], b_blocks, precision=highest
    )
    whole_block = jnp.exp(cumulative[:, -1, :])

    def advance(state_in, packed):
        block_state, block_decay = packed
        return (block_decay[:, None, None] * state_in + block_state, state_in)

    start = jnp.zeros((head_count, head_width, b_rows.shape[1]), values.dtype)
    _, entering = lax.scan(advance, start, (states, whole_block))
    outer = jnp.einsum("kin,khpn->kihp", c_blocks, entering, precision=highest)
    outer = outer * jnp.exp(cumulative)[:, :, :, None]
    output = (inner + outer).reshape(length, head_count, head_width)
    return output + skip[None, :, None] * values


def ssd_grads(values, dt_in, a_log, bias, skip, b_rows, c_rows, cotangent):

    def forward(value_arg, dt_arg):
        return ssd_group(value_arg, dt_arg, a_log, bias, skip, b_rows, c_rows)

    _, pullback = jax.vjp(forward, values, dt_in)
    return pullback(cotangent)


def body(grad_next, inputs, dt_raw, b_proj, c_proj, a_log, dt_bias, skip_gain):
    arriving = shifted(grad_next, "pipe", -1)
    length = inputs.shape[1]
    heads_here = a_log.shape[1]
    devices_per_group = lax.axis_size("tp") // G
    local_width = b_proj.shape[2] // G

    def spread_out(shard):
        by_group = jnp.transpose(shard.reshape(length, local_width, G), (0, 2, 1))
        return jnp.repeat(by_group, devices_per_group, axis=1)

    got_b, got_c = (
        lax.all_to_all(spread_out(b_proj[0]), "tp", split_axis=1, concat_axis=2, tiled=True),
        lax.all_to_all(spread_out(c_proj[0]), "tp", split_axis=1, concat_axis=2, tiled=True),
    )
    group_b = got_b.reshape(length, N).astype(jnp.float32)
    group_c = got_c.reshape(length, N).astype(jnp.float32)
    grad_x, grad_step = ssd_grads(
        inputs[0].astype(jnp.float32).reshape(length, heads_here, P_SIZE),
        dt_raw[0].astype(jnp.float32),
        a_log[0],
        dt_bias[0],
        skip_gain[0],
        group_b,
        group_c,
        arriving[0].astype(jnp.float32).reshape(length, heads_here, P_SIZE),
    )
    grad_cols = grad_x.reshape(length, heads_here * P_SIZE).astype(jnp.bfloat16)
    return (grad_cols[None], grad_step.astype(jnp.bfloat16)[None])


def solution(mesh):
    in_specs = (
        P("pipe", None, "tp"),
        P("pipe", None, "tp"),
        P("pipe", None, "tp"),
        P("pipe", None, "tp"),
        P("pipe", None, "tp"),
        P("pipe", "tp"),
        P("pipe", "tp"),
        P("pipe", "tp"),
    )
    out_specs = (P("pipe", None, "tp"), P("pipe", None, "tp"))
    return jax.shard_map(body, mesh=mesh, in_specs=in_specs, out_specs=out_specs, check_vma=False)
```

profile of v0, /device:TPU:0, one launch (start us, length us, event | category | flops | bytes accessed | tf_op | source)
XLA Modules:
  0.0 329.8 jit_solution(12946325112524738100)
XLA Ops:
  0.6 1.2 copy.128
  2.4 1.1 broadcast_in_dim.76
  3.5 7.4 %all-to-all-start.1 = ((bf16[2048,8,32]{0,2,1:T(8,128)(2,1)}), bf16[2048,8,32]{0,2,1:T(8,128)(2,1)S(1)}, u32[]{:S(2)}, u32[]{:S(2)}) async-start(bf16[2048,8,32]{0,2,1:T(8,128)(2,1)} %bitcast.10), calls=%async_computation.1 | async-start | bytes 2097152 | tf_op jit(solution)/shard_map/all_to_all | solution.py:72
  10.9 1.2 copy.123
  12.6 24.0 %all-to-all-done.1 = bf16[2048,8,32]{0,2,1:T(8,128)(2,1)S(1)} async-done(((bf16[2048,8,32]{0,2,1:T(8,128)(2,1)}), bf16[2048,8,32]{0,2,1:T(8,128)(2,1)S(1)}, u32[]{:S(2)}, u32[]{:S(2)}) %all-to-all-start.1) | async-done | bytes 1048608 | tf_op jit(solution)/shard_map/all_to_all | solution.py:72
  36.6 1.1 broadcast_in_dim.74
  37.7 4.3 %all-to-all-start = ((bf16[2048,8,32]{0,2,1:T(8,128)(2,1)}), bf16[2048,8,32]{0,2,1:T(8,128)(2,1)}, u32[]{:S(2)}, u32[]{:S(2)}) async-start(bf16[2048,8,32]{0,2,1:T(8,128)(2,1)} %bitcast.7), calls=%async_computation | async-start | bytes 2097152 | tf_op jit(solution)/shard_map/all_to_all | solution.py:73
  42.0 6.4 %copy.116 = bf16[1,2048,1024]{1,2,0:T(8,128)(2,1)} copy(bf16[1,2048,1024]{2,1,0:T(8,128)(2,1)} %param.12) | data formatting | bytes 8388608 | tf_op args[0]
  50.7 8.1 %reduce-window.14 = f32[8,16,2,128]{3,1,2,0:T(8,128)S(1)} reduce-window(f32[8,16,2,128]{3,1,2,0:T(8,128)} %bitcast.209, f32[]{:T(128)} %constant.81.clone.1), window={size=1x1x1x128 pad=0_0x0_0x0_0x127_0}, to_apply=%region_0.1 | reduce-window | flops 4161536 | bytes 262148 | tf_op jit(solution)/shard_map/reduce-window
  59.1 12.3 %reshape.258 = f32[8,256,16,64]{3,2,1,0:T(8,128)} reshape(bf16[1,2048,1024]{2,1,0:T(8,128)(2,1)} %param.13) | data formatting | bytes 12582912 | tf_op jit(solution)/shard_map/convert_element_type | solution.py:78
  71.5 13.9 %copy.127 = f32[8,256,16,64]{1,3,2,0:T(8,128)} copy(f32[8,256,16,64]{3,2,1,0:T(8,128)} %reshape.258) | data formatting | bytes 16777216 | tf_op jit(solution)/shard_map/convert_element_type | solution.py:78
  87.2 1.4 compare_select_fusion.3
  88.7 1.3 copy.172
  90.0 1.6 copy.150
  91.6 2.9 copy.171
  94.5 2.5 copy.149
  97.0 3.5 %fusion.37 = f32[8,256,256]{1,2,0:T(8,128)} fusion(bf16[8,256,256]{1,0,2:T(8,128)(2,1)} %bitcast.201, bf16[8,256,256]{1,0,2:T(8,128)(2,1)} %bitcast.203), kind=kOutput, calls=%fused_computation.50 | convolution fusion | flops 268435456 | bytes 4194304 | tf_op jit(solution)/shard_map/jvp(kin,kjn->kij)/dot_general | solution.py:27
  100.5 11.0 %fusion.19 = f32[8,16,64,256]{3,2,1,0:T(8,128)} fusion(bf16[8,256,256,1]{2,1,3,0:T(8,128)(2,1)S(1)} %copy.150, f32[8,256,16,64]{1,3,2,0:T(8,128)} %copy.127, f32[8,256,16]{1,2,0:T(8,128)} %get-tuple-element.268, f32[8,256,16]{1,2,0:T(8,128)} %get-tuple-element.265), kind=kOutput, calls=%fused_computation.36 | convolution fusion | flops 6446645248 | bytes 18087936 | tf_op jit(solution)/shard_map/jvp(kjhp,kjn->khpn)/dot_general | solution.py:34
  111.5 4.3 %broadcast.91.clone = f32[8,16,64,256]{3,2,1,0:T(8,128)} broadcast(f32[]{:T(128)} %constant.81.clone.1), dimensions={} | broadcast | bytes 8388612 | tf_op jit(solution)/shard_map/broadcast.6
  115.8 35.2 %while.34 = (s32[]{:T(128)}, f32[16,64,256]{2,1,0:T(8,128)S(1)}, f32[8,16,64,256]{3,2,1,0:T(8,128)}, f32[8,16,1,1]{1,3,2,0:T(1,128)}, f32[8,16]{1,0:T(8,128)}, /...) while((s32[]{:T(128)}, f32[16,64,256]{2,1,0:T(8,128)S(1)}, f32[8,16,64,256]{3,2,1,0:T(8,128)}, ...), condition=%wide.region_3.4_spmd.clone, body=%wide.region_2.3_spmd.clone.sunk | while | flops 1048579 | bytes 5245224 | solution.py:44
  115.8 1.2 bitcast_dynamic-update-slice_fusion.4
  117.6 1.4 bitcast_add_fusion.5
  119.0 1.2 constant_dynamic-update-slice_fusion.2
  122.0 1.4 bitcast_add_fusion.5
  123.4 1.2 constant_dynamic-update-slice_fusion.2
  126.4 1.4 bitcast_add_fusion.5
  127.8 1.2 constant_dynamic-update-slice_fusion.2
  130.7 1.4 bitcast_add_fusion.5
  132.2 1.2 constant_dynamic-update-slice_fusion.2
  133.4 1.1 bitcast_dynamic-update-slice_fusion.4
  135.2 1.4 bitcast_add_fusion.5
  136.6 1.2 constant_dynamic-update-slice_fusion.2
  139.6 1.4 bitcast_add_fusion.5
  141.0 1.2 constant_dynamic-update-slice_fusion.2
  142.2 1.1 bitcast_dynamic-update-slice_fusion.4
  144.0 1.4 bitcast_add_fusion.5
  145.4 1.2 constant_dynamic-update-slice_fusion.2
  146.6 1.1 bitcast_dynamic-update-slice_fusion.4
  148.4 1.4 bitcast_add_fusion.5
  149.8 1.2 constant_dynamic-update-slice_fusion.2
  151.0 3.8 %copy.169 = bf16[128,8,8,256]{3,2,1,0:T(8,128)(2,1)S(1)} copy(bf16[128,8,8,256]{3,1,2,0:T(8,128)(2,1)} %bitcast.45) | data formatting | bytes 8388608
  154.9 7.0 %fusion.14 = f32[8,16,64,256]{3,2,1,0:T(8,128)} fusion(bf16[8,256,256,1]{2,1,3,0:T(8,128)(2,1)S(1)} %copy-done.2, f32[8,256,16]{1,2,0:T(8,128)S(1)} %get-tuple-element.269, bf16[8,256,16,64]{1,0,3,2:T(8,128)(2,1)S(1)} %bitcast.194), kind=kOutput, calls=%fused_computation.26 | convolution fusion | flops 6446645248 | bytes 13762560 | tf_op jit(solution)/shard_map/transpose(jvp(kin,khpn->kihp))/dot_general | solution.py:45
  161.9 6.7 %fusion.15 = f32[8,256,16]{1,2,0:T(8,128)S(1)} fusion(f32[8,16,64,256]{3,2,1,0:T(8,128)S(1)} %bitcast.193, bf16[8,256,256,1]{2,1,3,0:T(8,128)(2,1)} %copy.149, bf16[8,256,16,64]{1,0,3,2:T(8,128)(2,1)S(1)} %bitcast.195), kind=kOutput, calls=%fused_computation.27 | convolution fusion | flops 6448709632 | bytes 13762560 | tf_op jit(solution)/shard_map/jvp(kin,khpn->kihp)/dot_general | solution.py:45
  168.6 4.3 %broadcast.91 = f32[8,16,64,256]{3,2,1,0:T(8,128)} broadcast(f32[]{:T(128)} %constant.81.clone.1), dimensions={} | broadcast | bytes 8388612 | tf_op jit(solution)/shard_map/broadcast.6
  172.8 29.3 %while.35 = (s32[]{:T(128)}, f32[16,64,256]{2,1,0:T(8,128)S(1)}, f32[8,16,64,256]{3,2,1,0:T(8,128)}, f32[8,16]{1,0:T(8,128)S(1)}, f32[8,16,64,256]{3,2,1,0:T(8,1...) while((s32[]{:T(128)}, f32[16,64,256]{2,1,0:T(8,128)S(1)}, ...), condition=%wide.region_6.7_spmd.clone, body=%wide.region_4.6_spmd.clone.sunk | while | flops 1572852 | bytes 6291980 | solution.py:44
  174.6 1.9 fusion.62
  176.5 1.1 bitcast_dynamic-update-slice_fusion.5
  178.3 1.9 fusion.62
  181.9 1.9 fusion.62
  183.8 1.1 bitcast_dynamic-update-slice_fusion.5
  185.6 1.9 fusion.62
  189.3 1.9 fusion.62
  192.9 1.9 fusion.62
  196.6 1.9 fusion.62
  198.5 1.2 bitcast_dynamic-update-slice_fusion.5
  200.3 1.9 fusion.62
  202.3 10.7 %fusion.50 = f32[8,16,64,256]{3,2,1,0:T(8,128)} fusion(f32[8,16,64,256]{3,2,1,0:T(8,128)} %get-tuple-element.179, bf16[8,256,256,1]{2,1,3,0:T(8,128)(2,1)S(1)} %copy-done.4), kind=kOutput, calls=%fused_computation.84 | convolution fusion | flops 6442450944 | bytes 17825792 | tf_op jit(solution)/shard_map/transpose(jvp(kjhp,kjn->khpn))/dot_general | solution.py:34
  213.0 30.5 %fusion.8 = (f32[8,256,16]{1,2,0:T(8,128)S(1)}, f32[8,256,16]{1,2,0:T(8,128)S(1)}) fusion(f32[8,256,16]{1,2,0:T(8,128)S(1)} %copy-done.11, f32[8,256,256]{1,2,0:T(8,128)S(1)} %copy-done.5, pred[256,256]{0,1:T(8,128)(4,1)S(1)} %iota_compare_fusion, bf16[8,256,16,64]{1,0,3,2:T(8,128)(2,1)S(1)} %bitcast.196, f32[8,256,16,64]{1,3,2,0:T(8,128)} %copy.127, ...), kind=kOutput, calls=%fused_computation.18 | convolution fusion | flops 6503202816 | bytes 15269888 | tf_op jit(solution)/shard_map/transpose(jvp(kijh,kjhp->kihp))/dot_general | solution.py:32
  243.6 28.1 %fusion.18 = (f32[8,256,16]{1,2,0:T(8,128)S(1)}, f32[8,256,16]{1,2,0:T(8,128)S(1)}, f32[8,256,16,64]{1,3,2,0:T(8,128)}) fusion(f32[8,16,64,256]{3,2,1,0:T(8,128)} %fusion.50, f32[8,256,16,64]{1,3,2,0:T(8,128)S(1)} %bitcast.199, f32[8,256,16]{1,2,0:T(8,128)S(1)} %copy-done.7, bf16[8,256,16,64]{1,0,3,2:T(8,128)(2,1)S(1)} %bitcast.197, ...), kind=kOutput, calls=%fused_computation.34 | convolution fusion | flops 6482231296 | bytes 32178176 | tf_op jit(solution)/shard_map/transpose(jvp(kijh,kjhp->kihp))/dot_general | solution.py:32
  272.3 19.9 %reduce-window.16 = f32[8,16,2,128]{3,1,2,0:T(8,128)S(1)} reduce-window(f32[8,16,2,128]{3,1,2,0:T(8,128)S(1)} %copy_bitcast_fusion, f32[]{:T(128)} %constant.81.clone.1), window={size=1x1x1x128 pad=0_0x0_0x0_0x0_127}, to_apply=%region_13.14 | reduce-window | flops 4161536 | bytes 262148 | tf_op jit(solution)/shard_map/reduce-window.2
  293.0 13.2 %copy.137 = f32[8,256,16,64]{1,0,3,2:T(8,128)} copy(f32[8,256,16,64]{1,3,2,0:T(8,128)} %get-tuple-element.270) | data formatting | bytes 16777216 | tf_op jit(solution)/shard_map/transpose(jvp(kijh,kjhp->kihp))/add_any | solution.py:32
  306.2 9.3 %reshape.246 = f32[1,2048,1024]{1,2,0:T(8,128)} reshape(f32[8,256,16,64]{1,0,3,2:T(8,128)} %copy.137) | data formatting | bytes 16777216 | tf_op jit(solution)/shard_map/transpose(jvp())/reshape | solution.py:24
  315.5 6.8 %fusion.17 = bf16[1,2048,1024]{1,2,0:T(8,128)(2,1)} fusion(f32[1,2048,1024]{1,2,0:T(8,128)} %reshape.246, bf16[1,2048,1024]{1,2,0:T(8,128)(2,1)} %collective-permute-done, f32[2048,16]{0,1:T(8,128)S(1)} %copy-done.9, f32[1024]{0:T(1024)S(1)} %mul.181), kind=kLoop, calls=%fused_computation.30 | loop fusion | flops 10485760 | bytes 16912384 | tf_op jit(solution)/shard_map/convert_element_type | solution.py:87
  322.3 6.4 %copy.148 = bf16[1,2048,1024]{2,1,0:T(8,128)(2,1)} copy(bf16[1,2048,1024]{1,2,0:T(8,128)(2,1)} %fusion.17) | data formatting | bytes 8388608
  (122 shorter events, 28.3 us)
Async XLA Ops:
  3.5 45.6 %copy-start.6 = (bf16[1,2048,16]{1,2,0:T(8,128)(2,1)S(1)}, bf16[1,2048,16]{1,2,0:T(8,128)(2,1)}, u32[]{:S(2)}) copy-start(bf16[1,2048,16]{1,2,0:T(8,128)(2,1)} %param.14) | copy-start | bytes 196612
  3.5 45.7 %copy-start.17 = (f32[1,16]{1,0:T(1,128)S(1)}, f32[1,16]{1,0:T(1,128)}, u32[]{:S(2)}) copy-start(f32[1,16]{1,0:T(1,128)} %param.17) | copy-start | bytes 196
  3.5 45.7 %copy-start.12 = (f32[1,16]{1,0:T(1,128)S(1)}, f32[1,16]{1,0:T(1,128)}, u32[]{:S(2)}) copy-start(f32[1,16]{1,0:T(1,128)} %param.18) | copy-start | bytes 196
  3.5 33.2 %all-to-all-start.1 = ((bf16[2048,8,32]{0,2,1:T(8,128)(2,1)}), bf16[2048,8,32]{0,2,1:T(8,128)(2,1)S(1)}, u32[]{:S(2)}, u32[]{:S(2)}) async-start(bf16[2048,8,32]{0,2,1:T(8,128)(2,1)} %bitcast.10), calls=%async_computation.1 | async-start | bytes 2097152 | tf_op jit(solution)/shard_map/all_to_all | solution.py:72
  37.7 53.9 %all-to-all-start = ((bf16[2048,8,32]{0,2,1:T(8,128)(2,1)}), bf16[2048,8,32]{0,2,1:T(8,128)(2,1)}, u32[]{:S(2)}, u32[]{:S(2)}) async-start(bf16[2048,8,32]{0,2,1:T(8,128)(2,1)} %bitcast.7), calls=%async_computation | async-start | bytes 2097152 | tf_op jit(solution)/shard_map/all_to_all | solution.py:73
  48.4 102.6 %collective-permute-start = (bf16[1,2048,1024]{1,2,0:T(8,128)(2,1)}, bf16[1,2048,1024]{1,2,0:T(8,128)(2,1)}, u32[]{:S(2)}, u32[]{:S(2)}) collective-permute-start(bf16[1,2048,1024]{1,2,0:T(8,128)(2,1)} %copy.116), channel_id=1, source_target_pairs={{0,24},{8,0},{16,8},{24,16},{1,25},{9,1},{17,9},{25,17},{2,26},{10... | collective-permute-start | bytes 12582920 | tf_op jit(solution)/shard_map/ppermute | solution.py:14
  49.2 1.5 copy-start.14
  71.4 14.8 %copy-start.16 = (f32[1,16]{1,0:T(1,128)S(1)}, f32[1,16]{1,0:T(1,128)}, u32[]{:S(2)}) copy-start(f32[1,16]{1,0:T(1,128)} %param.19) | copy-start | bytes 196
  85.5 0.9 copy-start.10
  91.6 19.9 %copy-start.3 = (bf16[8,256,256,1]{2,1,3,0:T(8,128)(2,1)}, bf16[8,256,256,1]{2,1,3,0:T(8,128)(2,1)S(1)}, u32[]{:S(2)}) copy-start(bf16[8,256,256,1]{2,1,3,0:T(8,128)(2,1)S(1)} %copy.150) | copy-start | bytes 3145732
  151.0 3.9 %copy-start.2 = (bf16[8,256,256,1]{2,1,3,0:T(8,128)(2,1)S(1)}, bf16[8,256,256,1]{2,1,3,0:T(8,128)(2,1)}, u32[]{:S(2)}) copy-start(bf16[8,256,256,1]{2,1,3,0:T(8,128)(2,1)} %copy.149) | copy-start | bytes 3145732
  151.0 10.9 %slice-start = ((s8[8388608]{0:T(1024)(128)(4,1)}), s8[4194304]{0:T(1024)(128)(4,1)S(1)}, s32[]{:S(2)}) async-start(s8[8388608]{0:T(1024)(128)(4,1)} %bitcast.192), calls=%async_computation.2 | async-start | bytes 8388608
  154.9 7.0 %copy-start = (bf16[128,8,8,256]{3,2,1,0:T(8,128)(2,1)}, bf16[128,8,8,256]{3,2,1,0:T(8,128)(2,1)S(1)}, u32[]{:S(2)}) copy-start(bf16[128,8,8,256]{3,2,1,0:T(8,128)(2,1)S(1)} %copy.169) | copy-start | bytes 12582916
  154.9 7.0 %slice-start.1 = ((s8[8388608]{0:T(1024)(128)(4,1)}), s8[4194304]{0:T(1024)(128)(4,1)S(1)}, s32[]{:S(2)}) async-start(s8[8388608]{0:T(1024)(128)(4,1)} %bitcast.192), calls=%async_computation.3 | async-start | bytes 8388608
  172.8 29.4 %copy-start.4 = (bf16[8,256,256,1]{2,1,3,0:T(8,128)(2,1)S(1)}, bf16[8,256,256,1]{2,1,3,0:T(8,128)(2,1)}, u32[]{:S(2)}) copy-start(bf16[8,256,256,1]{2,1,3,0:T(8,128)(2,1)} %copy-done.3) | copy-start | bytes 3145732
  202.2 10.8 %copy-start.1 = (bf16[128,8,8,256]{3,2,1,0:T(8,128)(2,1)S(1)}, bf16[128,8,8,256]{3,2,1,0:T(8,128)(2,1)}, u32[]{:S(2)}) copy-start(bf16[128,8,8,256]{3,2,1,0:T(8,128)(2,1)} %copy-done) | copy-start | bytes 12582916
  202.2 10.8 %copy-start.5 = (f32[8,256,256]{1,2,0:T(8,128)S(1)}, f32[8,256,256]{1,2,0:T(8,128)}, u32[]{:S(2)}) copy-start(f32[8,256,256]{1,2,0:T(8,128)} %fusion.37) | copy-start | bytes 6291460
  202.2 10.7 %copy-start.7 = (f32[8,256,16]{1,2,0:T(8,128)S(1)}, f32[8,256,16]{1,2,0:T(8,128)}, u32[]{:S(2)}) copy-start(f32[8,256,16]{1,2,0:T(8,128)} %get-tuple-element.265) | copy-start | bytes 393220
  202.2 10.7 %copy-start.11 = (f32[8,256,16]{1,2,0:T(8,128)S(1)}, f32[8,256,16]{1,2,0:T(8,128)}, u32[]{:S(2)}) copy-start(f32[8,256,16]{1,2,0:T(8,128)} %copy-done.10) | copy-start | bytes 393220
  202.3 41.3 %slice-start.2 = ((s8[8388608]{0:T(1024)(128)(4,1)}), s8[4194304]{0:T(1024)(128)(4,1)S(1)}, s32[]{:S(2)}) async-start(s8[8388608]{0:T(1024)(128)(4,1)} %bitcast.198), calls=%async_computation.4 | async-start | bytes 8388608
  213.0 30.6 %slice-start.3 = ((s8[8388608]{0:T(1024)(128)(4,1)}), s8[4194304]{0:T(1024)(128)(4,1)S(1)}, s32[]{:S(2)}) async-start(s8[8388608]{0:T(1024)(128)(4,1)} %bitcast.198), calls=%async_computation.5 | async-start | bytes 8388608
  213.0 30.6 %copy-start.8 = (f32[8,256,16]{1,2,0:T(8,128)S(1)}, f32[8,256,16]{1,2,0:T(8,128)}, u32[]{:S(2)}) copy-start(f32[8,256,16]{1,2,0:T(8,128)} %get-tuple-element.268) | copy-start | bytes 393220
  306.2 9.3 %copy-start.9 = (f32[2048,16]{0,1:T(8,128)S(1)}, f32[2048,16]{0,1:T(8,128)}, u32[]{:S(2)}) copy-start(f32[2048,16]{0,1:T(8,128)} %compare_select_fusion.3) | copy-start | bytes 393220
  322.3 6.4 %copy-start.13 = (f32[1,16]{1,0:T(1,128)S(1)}, f32[1,16]{1,0:T(1,128)}, u32[]{:S(2)}) copy-start(f32[1,16]{1,0:T(1,128)} %param.18) | copy-start | bytes 196
  322.3 6.4 %copy-start.15 = (f32[16]{0:T(128)S(1)}, f32[16]{0:T(128)}, u32[]{:S(2)}) copy-start(f32[16]{0:T(128)} %copy-done.14) | copy-start | bytes 196
where the time goes:
time: 335 us; the launch traced here: 330 us
  local copies, waits for them, and re-layouts  111 us (33%)
  matrix products  97.4 us (29%)
  other arithmetic  83.3 us (25%)
  waiting for transfers between devices  24 us (7%)
  starting transfers between devices  12.3 us (4%)
    dot_general x2, matrix products, ssd_group(): inner = jnp.einsum('kijh,kjhp->kihp', weights, scaled_x, precision=highest)  58.6 us
    another operation x7, other arithmetic  28.7 us
    convert_element_type x2, local copies, waits for them, and re-layouts, body(): inputs[0].astype(jnp.float32).reshape(length, heads_here, P_SIZE)  26.3 us
    all_to_all x1, waiting for transfers between devices, body(): lax.all_to_all(spread_out(b_proj[0]), 'tp', split_axis=1, concat_axis=2,...  24 us
    unnamed x52, local copies, waits for them, and re-layouts  23.5 us
    dot_general x2, matrix products, ssd_group(): jnp.einsum('kjhp,kjn->khpn', scaled_x * to_end[:, :, :, None], b_blocks,...  21.7 us
    dynamic_update_slice x16, other arithmetic, ssd_group(): _, entering = lax.scan(advance, start, (states, whole_block))  17.6 us
    reduce_sum x8, other arithmetic, advance(): return (block_decay[:, None, None] * state_in + block_state, state_in)  14.9 us
  transfers between devices with their start and end apart: 3, of which 1 were waited for; matrix products, arithmetic and copies ran while one was open for 33% of the time, Pallas kernels for 0%

commit v1 on v0

v1 whole, which is shorter than its diff:
```python
import functools

import jax
import jax.numpy as jnp
from jax import lax
from jax.experimental import pallas as pl
from jax.experimental.pallas import tpu as pltpu
from jax.sharding import PartitionSpec as P

P_SIZE = 64
N = 256
G = 4
SPAN = 256
COPIES = 3
CHUNKS = 4
F32, BF16 = jnp.float32, jnp.bfloat16


def dot(a, b):
    return jnp.dot(a, b, preferred_element_type=F32)


def split2(v):
    hi = v.astype(BF16)
    return hi, (v - hi.astype(F32)).astype(BF16)


def split3(v):
    hi = v.astype(BF16)
    rest = v - hi.astype(F32)
    mid = rest.astype(BF16)
    return hi, mid, (rest - mid.astype(F32)).astype(BF16)


def triangle(lower):
    row = lax.broadcasted_iota(jnp.int32, (SPAN, SPAN), 0)
    col = lax.broadcasted_iota(jnp.int32, (SPAN, SPAN), 1)
    return row >= col if lower else row <= col


def running(mask, v):
    ones = jnp.where(mask, 1.0, 0.0).astype(BF16)
    hi, mid, lo = split3(v)
    return dot(ones, hi) + dot(ones, mid) + dot(ones, lo)


def widen(v, onehot):
    hi, mid, lo = split3(v)
    part = lax.broadcasted_iota(jnp.int32, v.shape, 1) // (v.shape[1] // COPIES)
    parts = jnp.where(part == 0, hi.astype(F32), jnp.where(part == 1, mid.astype(F32), lo.astype(F32)))
    return dot(parts.astype(BF16), onehot)


def head_sum(v, onehot_t):
    hi, lo = split2(v)
    return dot(hi, onehot_t) + dot(lo, onehot_t)


def steps(raw, bias, rate):
    shifted_raw = raw.astype(F32) + bias
    near = jnp.exp(-jnp.abs(shifted_raw))
    step = jnp.maximum(shifted_raw, 0.0) + jnp.log1p(near)
    slope = jnp.where(shifted_raw >= 0, 1.0, near) / (1.0 + near)
    cum = running(triangle(True), rate * step)
    middle = 0.5 * cum[SPAN - 1 :, :]
    return step, slope, jnp.exp(cum - middle), jnp.exp(middle - cum), jnp.exp(middle)


def forward_kernel(raw, bias, rate, bt, ct, x, onehot, ybar, state):
    @pl.when(pl.program_id(0) == 0)
    def _():
        state[...] = jnp.zeros_like(state)

    step, _, _, fall, half = steps(raw[...], bias[...], rate[...])
    half_row = widen(jnp.broadcast_to(half, (8, half.shape[1])), onehot[...])[0:1]
    x_hi, x_lo = split2(x[...].astype(F32) * widen(step * fall, onehot[...]))
    c_rows = ct[...].T
    s_hi, s_lo = split2(jnp.where(triangle(True), dot(c_rows, bt[...]), 0.0))
    held = half_row * state[...]
    t_hi, t_lo = split2(held)
    ybar[...] = dot(s_hi, x_hi) + dot(s_hi, x_lo) + dot(s_lo, x_hi) + dot(c_rows, t_hi) + dot(c_rows, t_lo)
    state[...] = half_row * (held + dot(bt[...], x_hi) + dot(bt[...], x_lo))


def backward_kernel(
    raw, bias, rate, bt, ct, x, g, ybar, onehot, onehot_t, skip, state_in, carry_in, *rest
):
    grad_x, grad_dt, state, carry = rest[-4:]

    @pl.when(pl.program_id(0) == 0)
    def _():
        state[...] = state_in[...]
        carry[...] = carry_in[...]

    step, slope, rise, fall, _ = steps(raw[...], bias[...], rate[...])
    wide_rise = widen(rise, onehot[...])
    half_row = wide_rise[SPAN - 1 :, :]
    grad = g[...].astype(F32)
    g_hi, g_lo = split2(grad * wide_rise)
    b_rows = bt[...].T
    s_hi, s_lo = split2(jnp.where(triangle(False), dot(b_rows, ct[...]), 0.0))
    held = half_row * state[...]
    t_hi, t_lo = split2(held)
    zbar = dot(s_hi, g_hi) + dot(s_hi, g_lo) + dot(s_lo, g_hi) + dot(b_rows, t_hi) + dot(b_rows, t_lo)
    state[...] = half_row * (held + dot(ct[...], g_hi) + dot(ct[...], g_lo))
    grad_x[...] = (widen(step * fall, onehot[...]) * zbar + skip[...] * grad).astype(BF16)
    by_x = fall * head_sum(x[...].astype(F32) * zbar, onehot_t[...])
    by_y = rise * head_sum(grad * ybar[...], onehot_t[...])
    decay = running(triangle(False), by_y - step * by_x) + carry[0:1, :]
    carry[...] = jnp.broadcast_to(decay[0:1, :], carry.shape)
    heads = grad_dt.shape[1]
    grad_dt[...] = (slope * (by_x + rate[...] * decay))[:, :heads].astype(BF16)


def shifted(value, axis, by):
    length = lax.axis_size(axis)
    return lax.ppermute(value, axis, [(i, (i + by) % length) for i in range(length)])


def gather_rows(b_proj, c_proj):
    length, columns = b_proj.shape
    ways = lax.axis_size("tp")
    per_group = ways // G
    width = columns // G
    order = (jnp.arange(columns)[:, None] % width) * G + jnp.arange(columns)[:, None] // width
    pick = (order == jnp.arange(columns)[None, :]).astype(BF16)

    def turned(rows):
        return lax.dot_general(pick, rows, (((1,), (1,)), ((), ())), preferred_element_type=F32).astype(BF16)

    both = jnp.stack([turned(b_proj).reshape(G, width, length), turned(c_proj).reshape(G, width, length)], axis=1)
    strided = [[g * per_group + r for g in range(G)] for r in range(per_group)]
    mine = lax.all_to_all(both, "tp", 0, 0, axis_index_groups=strided, tiled=True)
    if per_group > 1:
        close = [[g * per_group + r for r in range(per_group)] for g in range(G)]
        mine = lax.all_gather(mine, "tp", axis=0, axis_index_groups=close, tiled=True)
    return mine[:, 0].reshape(N, length), mine[:, 1].reshape(N, length)


def body(grad_next, inputs, dt_raw, b_proj, c_proj, a_log, dt_bias, skip_gain):
    length, width = inputs.shape[1:]
    heads = a_log.shape[1]
    blocks = length // SPAN
    chunks = min(CHUNKS, blocks)
    per_chunk = blocks // chunks
    rows = length // chunks
    arriving = [shifted(grad_next[0, k * rows : (k + 1) * rows], "pipe", -1) for k in range(chunks - 1, -1, -1)]
    bt, ct = gather_rows(b_proj[0], c_proj[0])
    raw = jnp.tile(dt_raw[0], (1, COPIES))
    bias = jnp.tile(dt_bias, (1, COPIES))
    rate = -jnp.exp(jnp.tile(a_log, (1, COPIES)))
    skip = jnp.repeat(skip_gain, P_SIZE, axis=1)
    lanes = heads * COPIES
    onehot = (jnp.arange(lanes)[:, None] % heads == jnp.arange(width)[None, :] // P_SIZE).astype(BF16)
    onehot_t = (jnp.arange(lanes)[None, :] % heads == jnp.arange(width)[:, None] // P_SIZE).astype(BF16)
    x = inputs[0]

    def whole(shape):
        return pl.BlockSpec(shape, lambda k: (0, 0))

    def token_rows(columns, at):
        return pl.BlockSpec((SPAN, columns), lambda k: (at(k), 0))

    def token_cols(at):
        return pl.BlockSpec((N, SPAN), lambda k: (0, at(k)))

    params = pltpu.CompilerParams(vmem_limit_bytes=56 * 1024 * 1024, dimension_semantics=("arbitrary",))
    same = lambda k: k
    ybar = pl.pallas_call(
        forward_kernel,
        grid=(blocks,),
        in_specs=[
            token_rows(lanes, same),
            whole((1, lanes)),
            whole((1, lanes)),
            token_cols(same),
            token_cols(same),
            token_rows(width, same),
            whole((lanes, width)),
        ],
        out_specs=token_rows(width, same),
        out_shape=jax.ShapeDtypeStruct((length, width), F32),
        scratch_shapes=[pltpu.VMEM((N, width), F32)],
        compiler_params=params,
        cost_estimate=pl.CostEstimate(flops=18 * length * N * width, bytes_accessed=8 * length * width, transcendentals=0),
        name="states_forward",
    )(raw, bias, rate, bt, ct, x, onehot)

    state = jnp.zeros((N, width), F32)
    carry = jnp.zeros((8, lanes), F32)
    grads = ()
    for index, g in enumerate(arriving):
        base = (chunks - 1 - index) * per_chunk
        at = lambda k, base=base: base + per_chunk - 1 - k
        local = lambda k: per_chunk - 1 - k
        fixed = 13
        grad_x, grad_dt, state, carry = pl.pallas_call(
            backward_kernel,
            grid=(per_chunk,),
            in_specs=[
                token_rows(lanes, at),
                whole((1, lanes)),
                whole((1, lanes)),
                token_cols(at),
                token_cols(at),
                token_rows(width, at),
                token_rows(width, local),
                token_rows(width, at),
                whole((lanes, width)),
                whole((width, lanes)),
                whole((1, width)),
                whole((N, width)),
                whole((8, lanes)),
            ]
            + [pl.BlockSpec(memory_space=pl.ANY)] * len(grads),
            out_specs=[
                token_rows(width, at),
                token_rows(heads, at),
                whole((N, width)),
                whole((8, lanes)),
            ],
            out_shape=[
                jax.ShapeDtypeStruct((length, width), BF16),
                jax.ShapeDtypeStruct((length, heads), BF16),
                jax.ShapeDtypeStruct((N, width), F32),
                jax.ShapeDtypeStruct((8, lanes), F32),
            ],
            input_output_aliases={fixed: 0, fixed + 1: 1} if grads else {},
            compiler_params=params,
            cost_estimate=pl.CostEstimate(flops=30 * rows * N * width, bytes_accessed=12 * rows * width, transcendentals=0),
            name="gradients_%d" % index,
        )(raw, bias, rate, bt, ct, x, g, ybar, onehot, onehot_t, skip, state, carry, *grads)
        grads = (grad_x, grad_dt)
    return grads[0][None], grads[1][None]


def solution(mesh):
    wide, narrow = P("pipe", None, "tp"), P("pipe", "tp")
    return jax.shard_map(
        body,
        mesh=mesh,
        in_specs=(wide, wide, wide, wide, wide, narrow, narrow, narrow),
        out_specs=(wide, wide),
        check_vma=False,
    )
```

time: 335 us -> 141 us (0.42); the launches traced: 330 us -> 141 us
  local copies, waits for them, and re-layouts: 111 us -> 14.8 us
  matrix products: 97.4 us -> 1.73 us
  other arithmetic: 83.3 us -> 1.77 us
  Pallas kernels: 0 us -> 52.6 us
  blocking collectives: 0 us -> 31.9 us
  between operations: 1.33 us -> 14.2 us
  starting transfers between devices: 12.3 us -> 2.29 us
    dot_general x7 -> x2, matrix products: 97.4 us -> 1.73 us  [turned(): lax.dot_general(pick, rows, (((1,), (1,)), ((), ())), preferred_element_t...]
    pallas_call x0 -> x5, Pallas kernels: none -> 52.6 us  [the longest x4 35.6 us: body(): pl.pallas_call(backward_kernel, grid=(per_chunk,), in_specs=[token_rows(l...]
    all_to_all x0 -> x1, blocking collectives: none -> 31.9 us  [gather_rows(): lax.all_to_all(both, 'tp', 0, 0, axis_index_groups=strided, tiled=True)]
    another operation x7 -> x1, other arithmetic: 28.7 us -> 0.1 us  [gather_rows(): jnp.stack([turned(b_proj).reshape(G, width, length), turned(c_proj).resha...]
    convert_element_type x2 -> x0, local copies, waits for them, and re-layouts: 26.3 us -> none  [body(): inputs[0].astype(jnp.float32).reshape(length, heads_here, P_SIZE)]
    all_to_all x2 -> x0, waiting for transfers between devices: 24 us -> none  [the longest x1 24 us: body(): lax.all_to_all(spread_out(b_proj[0]), 'tp', split_axis=1, concat_axis=2,...]
    all_gather x0 -> x1, waiting for transfers between devices: none -> 21.4 us  [gather_rows(): lax.all_gather(mine, 'tp', axis=0, axis_index_groups=close, tiled=True)]
    unnamed x52 -> x13, local copies, waits for them, and re-layouts: 23.5 us -> 2.86 us
  transfers between devices with their start and end apart: 3 -> 5, of which waited for: 1 -> 1; matrix products, arithmetic and copies ran while one was open for 33% -> 10% of each run, Pallas kernels for 0% -> 31%
where the time goes in v1:
time: 141 us
  Pallas kernels  52.6 us (37%)
  blocking collectives  31.9 us (23%)
  waiting for transfers between devices  21.4 us (15%)
  local copies, waits for them, and re-layouts  14.8 us (10%)
  between operations  14.2 us (10%)
  starting transfers between devices  2.29 us (2%)
  other arithmetic  1.77 us (1%)
  matrix products  1.73 us (1%)
    pallas_call x4, Pallas kernels, body(): pl.pallas_call(backward_kernel, grid=(per_chunk,), in_specs=[token_rows(l...  35.6 us
    all_to_all x1, blocking collectives, gather_rows(): lax.all_to_all(both, 'tp', 0, 0, axis_index_groups=strided, tiled=True)  31.9 us
    all_gather x1, waiting for transfers between devices, gather_rows(): lax.all_gather(mine, 'tp', axis=0, axis_index_groups=close, tiled=True)  21.4 us
    pallas_call x1, Pallas kernels, body(): pl.pallas_call(forward_kernel, grid=(blocks,), in_specs=[token_rows(lanes...  17 us
    squeeze x1, local copies, waits for them, and re-layouts, body(): grad_next[0, k * rows:(k + 1) * rows]  3.99 us
    slice x1, local copies, waits for them, and re-layouts, gather_rows(): return (mine[:, 0].reshape(N, length), mine[:, 1].reshape(N, length))  3.12 us
    unnamed x13, local copies, waits for them, and re-layouts  2.86 us
  transfers between devices with their start and end apart: 5, of which 1 were waited for; matrix products, arithmetic and copies ran while one was open for 10% of the time, Pallas kernels for 31%

profile of v1, /device:TPU:0, one launch (start us, length us, event | category | flops | bytes accessed | tf_op | source)
XLA Modules:
  0.0 140.7 jit_solution(5366443524941080703)
XLA Ops:
  7.2 0.0 copy-start
  7.2 0.0 all-gather.2.cloned.1.call-start
  7.2 1.0 copy-done
  8.2 0.3 convolution_convert_fusion
  8.6 1.4 convolution_convert_fusion.1
  10.0 0.1 pad_maximum_fusion
  10.1 31.9 %all_to_all.5 = bf16[4,2,32,2048]{3,2,1,0:T(8,128)(2,1)} all-to-all(bf16[4,2,32,2048]{3,2,1,0:T(8,128)(2,1)S(1)} %pad_maximum_fusion), channel_id=1, replica_groups={{0,2,4,6},{1,3,5,7},{8,10,12,14},{9,11,13,15},{16,18,20,22},{17,19,21,2..., dimensions={0} | all-to-all | bytes 2097152 | tf_op jit(solution)/shard_map/all_to_all | solution.py:133
  42.0 0.0 all-gather.2.cloned.1.call-update
  42.0 0.0 copy-start.5
  42.0 0.0 copy-start.3
  42.1 0.0 copy-start.4
  42.1 0.0 copy-start.2
  42.1 4.0 %slice_bitcast_fusion = (bf16[512,1024]{1,0:T(8,128)(2,1)}, bf16[512,1024]{1,0:T(8,128)(2,1)}, bf16[512,1024]{1,0:T(8,128)(2,1)S(1)}, bf16[512,1024]{1,0:T(8,128)(2,1)}) fusion(bf16[1,2048,1024]{2,1,0:T(8,128)(2,1)} %param.8), kind=kLoop, calls=%fused_computation.3 | loop fusion | bytes 8388608 | tf_op jit(solution)/shard_map/squeeze | solution.py:147
  46.1 0.0 collective-permute-start.3
  46.1 1.6 %collective-permute-start.1 = (bf16[512,1024]{1,0:T(8,128)(2,1)}, bf16[512,1024]{1,0:T(8,128)(2,1)}, u32[]{:S(2)}, u32[]{:S(2)}) collective-permute-start(bf16[512,1024]{1,0:T(8,128)(2,1)} %get-tuple-element.39), channel_id=1, source_target_pairs={{0,24},{8,0},{16,8},{24,16},{1,25},{9,1},{17,9},{25,17},{2,26},{10... | collective-permute-start | bytes 3145736 | tf_op jit(solution)/shard_map/ppermute | solution.py:117
  47.7 0.0 collective-permute-start
  47.7 0.6 collective-permute-start.2
  48.3 0.0 copy-done.5
  48.3 0.6 neg.9.rate
  48.9 0.0 copy-done.3
  48.9 0.7 tile.33.bias
  49.6 0.0 copy-done.4
  49.6 0.1 broadcast_in_dim.24
  49.7 0.7 broadcast_in_dim.25.skip
  50.4 0.0 copy-done.2
  50.4 1.0 copy.38.raw
  51.4 0.7 compare_convert_fusion.1.onehot
  52.1 0.9 compare_convert_fusion.onehot_t
  53.1 21.4 %all-gather.2.cloned.1.call-done = bf16[8,2,32,2048]{3,2,1,0:T(8,128)(2,1)} async-done(((bf16[4,2,32,2048]{3,2,1,0:T(8,128)(2,1)}), bf16[8,2,32,2048]{3,2,1,0:T(8,128)(2,1)}) %all-gather.2.cloned.1.call-update) | async-done | bytes 2097168 | tf_op jit(solution)/shard_map/all_gather | solution.py:136
  74.4 3.1 %fusion.9 = (bf16[8,1,32,2048]{3,2,1,0:T(8,128)(2,1)}, bf16[8,1,32,2048]{3,2,1,0:T(8,128)(2,1)}) fusion(bf16[8,2,32,2048]{3,2,1,0:T(8,128)(2,1)} %all-gather.2.cloned.1.call-done), kind=kLoop, calls=%fused_computation.30 | loop fusion | bytes 4194304 | tf_op jit(solution)/shard_map/slice | solution.py:137
  77.5 17.0 %states_forward.1.ybar = f32[2048,1024]{1,0:T(8,128)} custom-call(bf16[2048,48]{1,0:T(8,128)(2,1)} %copy.38.raw, f32[1,48]{1,0:T(1,128)} %tile.33.bias, f32[1,48]{1,0:T(1,128)} %neg.9.rate, bf16[256,2048]{1,0:T(8,128)(2,1)} %bitcast.42, bf16[256,2048]{1,0:T(8,128)(2,1)} %bitcast.37, bf16[2048,1024]{1,0:T(8,128)(2,1)} %bitcast.31, ...), custom_call_target="tpu_custom_call" | custom-call | flops 9663676416 | bytes 16777216 | tf_op jit(solution)/shard_map/states_forward/pallas_call | solution.py:169
  94.5 0.0 collective-permute-done.3.g
  94.5 0.0 copy-start.1
  94.5 0.7 broadcast_in_dim.27.carry_in
  95.2 1.1 broadcast_in_dim.26.state_in
  96.3 0.0 copy-done.1
  96.3 8.8 %gradients_0.1 = (bf16[2048,1024]{1,0:T(8,128)(2,1)}, bf16[2048,16]{1,0:T(8,128)(2,1)}, f32[256,1024]{1,0:T(8,128)}, f32[8,48]{1,0:T(8,128)}) custom-call(bf16[2048,48]{1,0:T(8,128)(2,1)} %copy.38.raw, f32[1,48]{1,0:T(1,128)} %tile.33.bias, f32[1,48]{1,0:T(1,128)} %neg.9.rate, bf16[256,2048]{1,0:T(8,128)(2,1)} %bitcast.43, bf16[256,2048]{1,0:T(8,128)(2,1)} %bitcast.38, ...), custom_call_target="tpu_custom_call" | custom-call | flops 4026531840 | bytes 6291456 | tf_op jit(solution)/shard_map/gradients_0/pallas_call | solution.py:197
  105.2 0.0 collective-permute-done.2.g
  105.2 8.9 %gradients_1.1 = (bf16[2048,1024]{1,0:T(8,128)(2,1)}, bf16[2048,16]{1,0:T(8,128)(2,1)}, f32[256,1024]{1,0:T(8,128)}, f32[8,48]{1,0:T(8,128)}) custom-call(bf16[2048,48]{1,0:T(8,128)(2,1)} %copy.38.raw, f32[1,48]{1,0:T(1,128)} %tile.33.bias, f32[1,48]{1,0:T(1,128)} %neg.9.rate, ...), custom_call_target="tpu_custom_call", output_to_operand_aliasing={{0}: (13, {}), {1}: (14, {})} | custom-call | flops 4026531840 | bytes 6291456 | tf_op jit(solution)/shard_map/gradients_1/pallas_call | solution.py:197
  114.1 0.0 collective-permute-done.1.g
  114.1 8.9 %gradients_2.1 = (bf16[2048,1024]{1,0:T(8,128)(2,1)}, bf16[2048,16]{1,0:T(8,128)(2,1)}, f32[256,1024]{1,0:T(8,128)}, f32[8,48]{1,0:T(8,128)}) custom-call(bf16[2048,48]{1,0:T(8,128)(2,1)} %copy.38.raw, f32[1,48]{1,0:T(1,128)} %tile.33.bias, f32[1,48]{1,0:T(1,128)} %neg.9.rate, ...), custom_call_target="tpu_custom_call", output_to_operand_aliasing={{0}: (13, {}), {1}: (14, {})} | custom-call | flops 4026531840 | bytes 6291456 | tf_op jit(solution)/shard_map/gradients_2/pallas_call | solution.py:197
  122.9 0.0 collective-permute-done.g
  123.0 9.0 %gradients_3.1 = (bf16[2048,1024]{1,0:T(8,128)(2,1)}, bf16[2048,16]{1,0:T(8,128)(2,1)}, f32[256,1024]{1,0:T(8,128)}, f32[8,48]{1,0:T(8,128)}) custom-call(bf16[2048,48]{1,0:T(8,128)(2,1)} %copy.38.raw, f32[1,48]{1,0:T(1,128)} %tile.33.bias, f32[1,48]{1,0:T(1,128)} %neg.9.rate, ...), custom_call_target="tpu_custom_call", output_to_operand_aliasing={{0}: (13, {}), {1}: (14, {})} | custom-call | flops 4026531840 | bytes 6291456 | tf_op jit(solution)/shard_map/gradients_3/pallas_call | solution.py:197
  132.0 1.8 %copy.39 = bf16[1,2048,16]{1,2,0:T(8,128)(2,1)} copy(bf16[1,2048,16]{2,1,0:T(8,128)(2,1)} %bitcast.47) | data formatting | bytes 131072
  (7 shorter events, 0.0 us)
Async XLA Ops:
  7.2 1.0 copy-start
  7.2 67.2 %all-gather.2.cloned.1.call-start = ((), (), s32[]{:S(2)}) async-start(), calls=%async_computation.1 | async-start | bytes 3145728 | tf_op jit(solution)/shard_map/all_gather | solution.py:136
  42.0 6.3 %copy-start.5 = (f32[1,16]{1,0:T(1,128)S(1)}, f32[1,16]{1,0:T(1,128)}, u32[]{:S(2)}) copy-start(f32[1,16]{1,0:T(1,128)} %param.13) | copy-start | bytes 196
  42.0 6.9 %copy-start.3 = (f32[1,16]{1,0:T(1,128)S(1)}, f32[1,16]{1,0:T(1,128)}, u32[]{:S(2)}) copy-start(f32[1,16]{1,0:T(1,128)} %param.14) | copy-start | bytes 196
  42.1 7.6 %copy-start.4 = (f32[1,16]{1,0:T(1,128)S(1)}, f32[1,16]{1,0:T(1,128)}, u32[]{:S(2)}) copy-start(f32[1,16]{1,0:T(1,128)} %param.15) | copy-start | bytes 196
  42.1 8.3 %copy-start.2 = (bf16[1,2048,16]{1,2,0:T(8,128)(2,1)S(1)}, bf16[1,2048,16]{1,2,0:T(8,128)(2,1)}, u32[]{:S(2)}) copy-start(bf16[1,2048,16]{1,2,0:T(8,128)(2,1)} %param.10) | copy-start | bytes 196612
  46.1 48.5 %collective-permute-start.3 = (bf16[512,1024]{1,0:T(8,128)(2,1)}, bf16[512,1024]{1,0:T(8,128)(2,1)S(1)}, u32[]{:S(2)}, u32[]{:S(2)}) collective-permute-start(bf16[512,1024]{1,0:T(8,128)(2,1)} %get-tuple-element.38), channel_id=1, source_target_pairs={{0,24},{8,0},{16,8},{24,16},{1,25},{9,1},{17,9},{25,17},{2,26},{10... | collective-permute-start | bytes 3145736 | tf_op jit(solution)/shard_map/ppermute | solution.py:117
  46.1 68.0 %collective-permute-start.1 = (bf16[512,1024]{1,0:T(8,128)(2,1)}, bf16[512,1024]{1,0:T(8,128)(2,1)}, u32[]{:S(2)}, u32[]{:S(2)}) collective-permute-start(bf16[512,1024]{1,0:T(8,128)(2,1)} %get-tuple-element.39), channel_id=1, source_target_pairs={{0,24},{8,0},{16,8},{24,16},{1,25},{9,1},{17,9},{25,17},{2,26},{10... | collective-permute-start | bytes 3145736 | tf_op jit(solution)/shard_map/ppermute | solution.py:117
  47.7 75.2 %collective-permute-start = (bf16[512,1024]{1,0:T(8,128)(2,1)S(1)}, bf16[512,1024]{1,0:T(8,128)(2,1)}, u32[]{:S(2)}, u32[]{:S(2)}) collective-permute-start(bf16[512,1024]{1,0:T(8,128)(2,1)S(1)} %get-tuple-element.40), channel_id=1, source_target_pairs={{0,24},{8,0},{16,8},{24,16},{1,25},{9,1},{17,9},{25,17},{2,26},{10... | collective-permute-start | bytes 3145736 | tf_op jit(solution)/shard_map/ppermute | solution.py:117
  47.7 57.4 %collective-permute-start.2 = (bf16[512,1024]{1,0:T(8,128)(2,1)}, bf16[512,1024]{1,0:T(8,128)(2,1)}, u32[]{:S(2)}, u32[]{:S(2)}) collective-permute-start(bf16[512,1024]{1,0:T(8,128)(2,1)} %get-tuple-element.41), channel_id=1, source_target_pairs={{0,24},{8,0},{16,8},{24,16},{1,25},{9,1},{17,9},{25,17},{2,26},{10... | collective-permute-start | bytes 3145736 | tf_op jit(solution)/shard_map/ppermute | solution.py:117
  94.5 1.8 %copy-start.1 = (bf16[512,1024]{1,0:T(8,128)(2,1)}, bf16[512,1024]{1,0:T(8,128)(2,1)S(1)}, u32[]{:S(2)}) copy-start(bf16[512,1024]{1,0:T(8,128)(2,1)S(1)} %collective-permute-done.3.g) | copy-start | bytes 3145732
Sparse Core Ops, SparseCore 0:
  42.2 32.2 all-gather.1

commit v2 on v1

--- a/solution.py
+++ b/solution.py
@@ -1,3 +1,5 @@
+import functools
+
 import functools
 
 import jax
@@ -64,6 +66,89 @@
     cum = running(triangle(True), rate * step)
     middle = 0.5 * cum[SPAN - 1 :, :]
     return step, slope, jnp.exp(cum - middle), jnp.exp(middle - cum), jnp.exp(middle)
+
+
+def forward_sends(blocks, per_group, raw, bias, rate, out, x, onehot, ybar, bt, ct, state, land, send1, recv1, send2, recv2):
+    now = pl.program_id(0)
+    me = lax.axis_index("tp")
+    group, place = me // per_group, me % per_group
+
+    def across(j, d):
+        to = (group + d) % G
+        return pltpu.make_async_remote_copy(
+            src_ref=out.at[j, to],
+            dst_ref=land.at[j, place, group],
+            send_sem=send1.at[j, d],
+            recv_sem=recv1.at[j, d],
+            device_id={"tp": to * per_group + place},
+            device_id_type=pl.DeviceIdType.MESH,
+        )
+
+    def beside(j, d):
+        return pltpu.make_async_remote_copy(
+            src_ref=land.at[j, place],
+            dst_ref=land.at[j, place],
+            send_sem=send2.at[j, d],
+            recv_sem=recv2.at[j, d],
+            device_id={"tp": group * per_group + (place + d) % per_group},
+            device_id_type=pl.DeviceIdType.MESH,
+        )
+
+    def own(j):
+        return pltpu.make_async_copy(out.at[j, group], land.at[j, place, group], recv1.at[j, 0])
+
+    def pass_on(j):
+        own(j).wait()
+        for d in range(1, G):
+            across(j, d).wait_recv()
+        for d in range(1, per_group):
+            beside(j, d).start()
+
+    @pl.when(now == 0)
+    def _():
+        barrier = pltpu.get_barrier_semaphore()
+        for d in range(1, G):
+            pl.semaphore_signal(
+                barrier,
+                inc=1,
+                device_id={"tp": (group + d) % G * per_group + place},
+                device_id_type=pl.DeviceIdType.MESH,
+            )
+        for d in range(1, per_group):
+            pl.semaphore_signal(
+                barrier,
+                inc=1,
+                device_id={"tp": group * per_group + (place + d) % per_group},
+                device_id_type=pl.DeviceIdType.MESH,
+            )
+        pl.semaphore_wait(barrier, G - 1 + per_group - 1)
+
+        @pl.loop(0, blocks)
+        def _(j):
+            own(j).start()
+            for d in range(1, G):
+                across(j, d).start()
+
+        pass_on(0)
+
+    @pl.when(now + 1 < blocks)
+    def _():
+        pass_on(now + 1)
+
+    for d in range(1, per_group):
+        beside(now, d).wait_recv()
+    bt[...] = land[now, :, :, 0].reshape(N, SPAN)
+    ct[...] = land[now, :, :, 1].reshape(N, SPAN)
+    forward_kernel(raw, bias, rate, bt, ct, x, onehot, ybar, state)
+
+    @pl.when(now == blocks - 1)
+    def _():
+        @pl.loop(0, blocks)
+        def _(j):
+            for d in range(1, G):
+                across(j, d).wait_send()
+            for d in range(1, per_group):
+                beside(j, d).wait_send()
 
 
 def forward_kernel(raw, bias, rate, bt, ct, x, onehot, ybar, state):
@@ -117,6 +202,20 @@
     return lax.ppermute(value, axis, [(i, (i + by) % length) for i in range(length)])
 
 
+def outgoing(b_proj, c_proj):
+    length, columns = b_proj.shape
+    width = columns // G
+    blocks = length // SPAN
+    kind = jnp.arange(2 * columns) // width % 2
+    entry = jnp.arange(2 * columns) // (2 * width) + jnp.arange(2 * columns) % width * G
+    take = jnp.arange(columns)[None, :]
+    sides = [((entry[:, None] == take) & (kind[:, None] == which)).astype(BF16) for which in range(2)]
+    pick = jnp.concatenate(sides, axis=1)
+    rows = jnp.concatenate([b_proj, c_proj], axis=1).reshape(blocks, SPAN, 2 * columns)
+    turned = jnp.einsum("cd,ktd->kct", pick, rows, preferred_element_type=F32).astype(BF16)
+    return turned.reshape(blocks, G, 2, width, SPAN)
+
+
 def gather_rows(b_proj, c_proj):
     length, columns = b_proj.shape
     ways = lax.axis_size("tp")
@@ -145,7 +244,9 @@
     per_chunk = blocks // chunks
     rows = length // chunks
     arriving = [shifted(grad_next[0, k * rows : (k + 1) * rows], "pipe", -1) for k in range(chunks - 1, -1, -1)]
-    bt, ct = gather_rows(b_proj[0], c_proj[0])
+    per_group = lax.axis_size("tp") // G
+    entries = b_proj.shape[2] // G
+    fused = entries % 16 == 0
     raw = jnp.tile(dt_raw[0], (1, COPIES))
     bias = jnp.tile(dt_bias, (1, COPIES))
     rate = -jnp.exp(jnp.tile(a_log, (1, COPIES)))
@@ -166,25 +267,63 @@
 
     params = pltpu.CompilerParams(vmem_limit_bytes=56 * 1024 * 1024, dimension_semantics=("arbitrary",))
     same = lambda k: k
-    ybar = pl.pallas_call(
-        forward_kernel,
-        grid=(blocks,),
-        in_specs=[
-            token_rows(lanes, same),
-            whole((1, lanes)),
-            whole((1, lanes)),
-            token_cols(same),
-            token_cols(same),
-            token_rows(width, same),
-            whole((lanes, width)),
-        ],
-        out_specs=token_rows(width, same),
-        out_shape=jax.ShapeDtypeStruct((length, width), F32),
-        scratch_shapes=[pltpu.VMEM((N, width), F32)],
-        compiler_params=params,
-        cost_estimate=pl.CostEstimate(flops=18 * length * N * width, bytes_accessed=8 * length * width, transcendentals=0),
-        name="states_forward",
-    )(raw, bias, rate, bt, ct, x, onehot)
+    cost = pl.CostEstimate(flops=18 * length * N * width, bytes_accessed=8 * length * width, transcendentals=0)
+    if fused:
+        ybar, bt, ct = pl.pallas_call(
+            functools.partial(forward_sends, blocks, per_group),
+            grid=(blocks,),
+            in_specs=[
+                token_rows(lanes, same),
+                whole((1, lanes)),
+                whole((1, lanes)),
+                pl.BlockSpec(memory_space=pl.ANY),
+                token_rows(width, same),
+                whole((lanes, width)),
+            ],
+            out_specs=[token_rows(width, same), token_cols(same), token_cols(same)],
+            out_shape=[
+                jax.ShapeDtypeStruct((length, width), F32),
+                jax.ShapeDtypeStruct((N, length), BF16),
+                jax.ShapeDtypeStruct((N, length), BF16),
+            ],
+            scratch_shapes=[
+                pltpu.VMEM((N, width), F32),
+                pltpu.VMEM((blocks, per_group, G, 2, entries, SPAN), BF16),
+                pltpu.SemaphoreType.DMA((blocks, G)),
+                pltpu.SemaphoreType.DMA((blocks, G)),
+                pltpu.SemaphoreType.DMA((blocks, per_group)),
+                pltpu.SemaphoreType.DMA((blocks, per_group)),
+            ],
+            compiler_params=pltpu.CompilerParams(
+                vmem_limit_bytes=40 * 1024 * 1024,
+                dimension_semantics=("arbitrary",),
+                collective_id=0,
+                has_side_effects=True,
+            ),
+            cost_estimate=cost,
+            name="exchange_forward",
+        )(raw, bias, rate, outgoing(b_proj[0], c_proj[0]), x, onehot)
+    else:
+        bt, ct = gather_rows(b_proj[0], c_proj[0])
+        ybar = pl.pallas_call(
+            forward_kernel,
+            grid=(blocks,),
+            in_specs=[
+                token_rows(lanes, same),
+                whole((1, lanes)),
+                whole((1, lanes)),
+                token_cols(same),
+                token_cols(same),
+                token_rows(width, same),
+                whole((lanes, width)),
+            ],
+            out_specs=token_rows(width, same),
+            out_shape=jax.ShapeDtypeStruct((length, width), F32),
+            scratch_shapes=[pltpu.VMEM((N, width), F32)],
+            compiler_params=params,
+            cost_estimate=cost,
+            name="states_forward",
+        )(raw, bias, rate, bt, ct, x, onehot)
 
     state = jnp.zeros((N, width), F32)
     carry = jnp.zeros((8, lanes), F32)

time: 141 us -> 98.6 us (0.70)
  blocking collectives: 31.9 us -> 0 us
  Pallas kernels: 52.6 us -> 78.7 us
  waiting for transfers between devices: 21.4 us -> 0.01 us
  between operations: 14.2 us -> 0.86 us
  local copies, waits for them, and re-layouts: 14.8 us -> 12.9 us
    all_to_all x1 -> x0, blocking collectives: 31.9 us -> none  [gather_rows(): lax.all_to_all(both, 'tp', 0, 0, axis_index_groups=strided, tiled=True)]
    pallas_call x1, Pallas kernels: 17 us -> 43 us  [body(): pl.pallas_call(functools.partial(forward_sends, blocks, per_group), grid=...]
    all_gather x1 -> x0, waiting for transfers between devices: 21.4 us -> none  [gather_rows(): lax.all_gather(mine, 'tp', axis=0, axis_index_groups=close, tiled=True)]
    unnamed x13 -> x27, local copies, waits for them, and re-layouts: 2.86 us -> 6.04 us
    slice x1 -> x0, local copies, waits for them, and re-layouts: 3.12 us -> none  [gather_rows(): return (mine[:, 0].reshape(N, length), mine[:, 1].reshape(N, length))]
  transfers between devices with their start and end apart: 5 -> 4, of which waited for: 1 -> 0; matrix products, arithmetic and copies ran while one was open for 10% -> 6% of each run, Pallas kernels for 31% -> 71%
where the time goes in v2:
time: 98.6 us; the launch traced here: 98.3 us
  Pallas kernels  78.7 us (80%)
  local copies, waits for them, and re-layouts  12.9 us (13%)
  starting transfers between devices  3.14 us (3%)
  matrix products  1.52 us (2%)
  other arithmetic  1.19 us (1%)
    pallas_call x1, Pallas kernels, body(): pl.pallas_call(functools.partial(forward_sends, blocks, per_group), grid=...  43 us
    pallas_call x4, Pallas kernels, body(): pl.pallas_call(backward_kernel, grid=(per_chunk,), in_specs=[token_rows(l...  35.7 us
    unnamed x27, local copies, waits for them, and re-layouts  6.04 us
    squeeze x1, local copies, waits for them, and re-layouts, body(): grad_next[0, k * rows:(k + 1) * rows]  3.98 us
    ppermute x4, starting transfers between devices, shifted(): lax.ppermute(value, axis, [(i, (i + by) % length) for i in range(length)])  3.14 us
  transfers between devices with their start and end apart: 4, of which 0 were waited for; matrix products, arithmetic and copies ran while one was open for 6% of the time, Pallas kernels for 71%

profile of v2, /device:TPU:0, one launch (start us, length us, event | category | flops | bytes accessed | tf_op | source)
XLA Modules:
  0.0 98.3 jit_solution(4030740503308505224)
XLA Ops:
  0.6 0.0 copy-start.12
  0.6 0.0 copy-start.9
  0.7 0.0 copy-start.8
  0.7 0.0 copy-start.11
  0.7 4.0 %slice_bitcast_fusion = (bf16[512,1024]{1,0:T(8,128)(2,1)}, bf16[512,1024]{1,0:T(8,128)(2,1)}, bf16[512,1024]{1,0:T(8,128)(2,1)S(1)}, bf16[512,1024]{1,0:T(8,128)(2,1)}) fusion(bf16[1,2048,1024]{2,1,0:T(8,128)(2,1)} %param.8), kind=kLoop, calls=%fused_computation.4 | loop fusion | bytes 8388608 | tf_op jit(solution)/shard_map/squeeze | solution.py:246
  4.7 2.4 %collective-permute-start.3 = (bf16[512,1024]{1,0:T(8,128)(2,1)}, bf16[512,1024]{1,0:T(8,128)(2,1)S(1)}, u32[]{:S(2)}, u32[]{:S(2)}) collective-permute-start(bf16[512,1024]{1,0:T(8,128)(2,1)} %get-tuple-element.40), channel_id=1, source_target_pairs={{0,24},{8,0},{16,8},{24,16},{1,25},{9,1},{17,9},{25,17},{2,26},{10... | collective-permute-start | bytes 3145736 | tf_op jit(solution)/shard_map/ppermute | solution.py:202
  7.1 0.7 collective-permute-start.1
  7.7 0.0 collective-permute-start
  7.8 0.0 collective-permute-start.2
  7.8 0.0 copy-done.12
  7.9 0.1 neg.9.rate
  7.9 0.0 copy-start.5
  7.9 0.0 copy-done.9
  7.9 0.1 tile.33.bias
  8.0 0.0 copy-start.6
  8.0 0.0 copy-done.8
  8.1 0.3 copy.22.raw
  8.3 0.0 copy-start.3
  8.3 0.1 compare_convert_fusion.1.onehot
  8.4 0.0 copy-start.4
  8.4 0.2 fusion.6
  8.6 0.0 copy-done.11
  8.6 1.5 %convolution_convert_fusion = bf16[8,256,256]{1,2,0:T(8,128)(2,1)S(1)} fusion(bf16[8,256,128]{2,1,0:T(8,128)(2,1)S(1)} %bitcast.37, bf16[8,256,128]{2,1,0:T(8,128)(2,1)} %bitcast.38, pred[256,128]{1,0:T(32,128)(4,1)S(1)} %get-tuple-element.45, pred[256,128]{1,0:T(32,128)(4,1)S(1)} %get-tuple-element.44), kind=kOutput, calls=%fused_computation | convolution fusion | flops 271122432 | bytes 2162688 | tf_op jit(solution)/shard_map/cd,ktd->kct/dot_general | solution.py:215
  10.2 0.0 copy-start
  10.2 2.2 %copy-done = bf16[1,2048,1024]{2,1,0:T(8,128)(2,1)S(1)} copy-done((bf16[1,2048,1024]{2,1,0:T(8,128)(2,1)S(1)}, bf16[1,2048,1024]{2,1,0:T(8,128)(2,1)}, u32[]{:S(2)}) %copy-start) | copy-done | bytes 4194328
  12.4 0.0 copy-start.10
  12.4 43.0 %exchange_forward.1 = (f32[2048,1024]{1,0:T(8,128)}, bf16[256,2048]{1,0:T(8,128)(2,1)S(1)}, bf16[256,2048]{1,0:T(8,128)(2,1)S(1)}) custom-call(bf16[2048,48]{1,0:T(8,128)(2,1)S(1)} %copy.22.raw, f32[1,48]{1,0:T(1,128)S(1)} %tile.33.bias, f32[1,48]{1,0:T(1,128)S(1)} %neg.9.rate, bf16[8,4,2,32,256]{4,3,2,1,0:T(8,128)(2,1)S(1)} %bitcast.30, ...), custom_call_target="tpu_custom_call" | custom-call | flops 9663676416 | bytes 16777216 | tf_op jit(solution)/shard_map/exchange_forward/pallas_call | solution.py:272
  55.4 0.0 copy-done.5
  55.4 0.0 copy-done.6
  55.4 0.0 copy-done.3
  55.4 0.0 copy-done.4
  55.4 0.0 copy-start.1
  55.4 1.0 copy-done.1
  56.4 0.0 copy-start.2
  56.4 1.0 copy-done.2
  57.4 0.0 copy-done.10
  57.4 0.1 broadcast_in_dim.12
  57.5 0.7 broadcast_in_dim.13.skip
  58.2 0.9 compare_convert_fusion.onehot_t
  59.1 0.0 collective-permute-done.3.g
  59.1 0.0 copy-start.7
  59.1 0.6 broadcast_in_dim.29.carry_in
  59.7 1.1 %broadcast_in_dim.28.state_in = f32[256,1024]{1,0:T(8,128)} broadcast(f32[]{:T(128)} %constant.108.clone.1), dimensions={} | broadcast | bytes 1048580 | tf_op jit(solution)/shard_map/broadcast_in_dim | solution.py:328
  60.8 0.0 copy-done.7
  60.8 8.9 %gradients_0.1 = (bf16[2048,1024]{1,0:T(8,128)(2,1)}, bf16[2048,16]{1,0:T(8,128)(2,1)}, f32[256,1024]{1,0:T(8,128)}, f32[8,48]{1,0:T(8,128)}) custom-call(bf16[2048,48]{1,0:T(8,128)(2,1)} %copy-done.3, f32[1,48]{1,0:T(1,128)} %copy-done.6, f32[1,48]{1,0:T(1,128)} %copy-done.5, bf16[256,2048]{1,0:T(8,128)(2,1)} %copy-done.1, bf16[256,2048]{1,0:T(8,128)(2,1)} %copy-done.2, ...), custom_call_target="tpu_custom_call" | custom-call | flops 4026531840 | bytes 6291456 | tf_op jit(solution)/shard_map/gradients_0/pallas_call | solution.py:336
  69.6 0.0 collective-permute-done.2.g
  69.7 8.9 %gradients_1.1 = (bf16[2048,1024]{1,0:T(8,128)(2,1)}, bf16[2048,16]{1,0:T(8,128)(2,1)}, f32[256,1024]{1,0:T(8,128)}, f32[8,48]{1,0:T(8,128)}) custom-call(bf16[2048,48]{1,0:T(8,128)(2,1)} %copy-done.3, f32[1,48]{1,0:T(1,128)} %copy-done.6, f32[1,48]{1,0:T(1,128)} %copy-done.5, ...), custom_call_target="tpu_custom_call", output_to_operand_aliasing={{0}: (13, {}), {1}: (14, {})} | custom-call | flops 4026531840 | bytes 6291456 | tf_op jit(solution)/shard_map/gradients_1/pallas_call | solution.py:336
  78.5 0.0 collective-permute-done.1.g
  78.5 8.9 %gradients_2.1 = (bf16[2048,1024]{1,0:T(8,128)(2,1)}, bf16[2048,16]{1,0:T(8,128)(2,1)}, f32[256,1024]{1,0:T(8,128)}, f32[8,48]{1,0:T(8,128)}) custom-call(bf16[2048,48]{1,0:T(8,128)(2,1)} %copy-done.3, f32[1,48]{1,0:T(1,128)} %copy-done.6, f32[1,48]{1,0:T(1,128)} %copy-done.5, ...), custom_call_target="tpu_custom_call", output_to_operand_aliasing={{0}: (13, {}), {1}: (14, {})} | custom-call | flops 4026531840 | bytes 6291456 | tf_op jit(solution)/shard_map/gradients_2/pallas_call | solution.py:336
  87.4 0.0 collective-permute-done.g
  87.4 9.0 %gradients_3.1 = (bf16[2048,1024]{1,0:T(8,128)(2,1)}, bf16[2048,16]{1,0:T(8,128)(2,1)}, f32[256,1024]{1,0:T(8,128)}, f32[8,48]{1,0:T(8,128)}) custom-call(bf16[2048,48]{1,0:T(8,128)(2,1)} %copy-done.3, f32[1,48]{1,0:T(1,128)} %copy-done.6, f32[1,48]{1,0:T(1,128)} %copy-done.5, ...), custom_call_target="tpu_custom_call", output_to_operand_aliasing={{0}: (13, {}), {1}: (14, {})} | custom-call | flops 4026531840 | bytes 6291456 | tf_op jit(solution)/shard_map/gradients_3/pallas_call | solution.py:336
  96.5 1.8 %copy.23 = bf16[1,2048,16]{1,2,0:T(8,128)(2,1)} copy(bf16[1,2048,16]{2,1,0:T(8,128)(2,1)} %bitcast.32) | data formatting | bytes 131072
  (8 shorter events, 0.0 us)
Async XLA Ops:
  0.6 7.2 %copy-start.12 = (f32[1,16]{1,0:T(1,128)S(1)}, f32[1,16]{1,0:T(1,128)}, u32[]{:S(2)}) copy-start(f32[1,16]{1,0:T(1,128)} %param.13) | copy-start | bytes 196
  0.6 7.3 %copy-start.9 = (f32[1,16]{1,0:T(1,128)S(1)}, f32[1,16]{1,0:T(1,128)}, u32[]{:S(2)}) copy-start(f32[1,16]{1,0:T(1,128)} %param.14) | copy-start | bytes 196
  0.7 7.4 %copy-start.8 = (bf16[1,2048,16]{1,2,0:T(8,128)(2,1)S(1)}, bf16[1,2048,16]{1,2,0:T(8,128)(2,1)}, u32[]{:S(2)}) copy-start(bf16[1,2048,16]{1,2,0:T(8,128)(2,1)} %param.10) | copy-start | bytes 196612
  0.7 8.0 %copy-start.11 = (bf16[1,2048,128]{2,1,0:T(8,128)(2,1)S(1)}, bf16[1,2048,128]{2,1,0:T(8,128)(2,1)}, u32[]{:S(2)}) copy-start(bf16[1,2048,128]{2,1,0:T(8,128)(2,1)} %param.12) | copy-start | bytes 1572868
  4.7 54.4 %collective-permute-start.3 = (bf16[512,1024]{1,0:T(8,128)(2,1)}, bf16[512,1024]{1,0:T(8,128)(2,1)S(1)}, u32[]{:S(2)}, u32[]{:S(2)}) collective-permute-start(bf16[512,1024]{1,0:T(8,128)(2,1)} %get-tuple-element.40), channel_id=1, source_target_pairs={{0,24},{8,0},{16,8},{24,16},{1,25},{9,1},{17,9},{25,17},{2,26},{10... | collective-permute-start | bytes 3145736 | tf_op jit(solution)/shard_map/ppermute | solution.py:202
  7.1 71.5 %collective-permute-start.1 = (bf16[512,1024]{1,0:T(8,128)(2,1)}, bf16[512,1024]{1,0:T(8,128)(2,1)}, u32[]{:S(2)}, u32[]{:S(2)}) collective-permute-start(bf16[512,1024]{1,0:T(8,128)(2,1)} %get-tuple-element.41), channel_id=1, source_target_pairs={{0,24},{8,0},{16,8},{24,16},{1,25},{9,1},{17,9},{25,17},{2,26},{10... | collective-permute-start | bytes 3145736 | tf_op jit(solution)/shard_map/ppermute | solution.py:202
  7.7 79.7 %collective-permute-start = (bf16[512,1024]{1,0:T(8,128)(2,1)S(1)}, bf16[512,1024]{1,0:T(8,128)(2,1)}, u32[]{:S(2)}, u32[]{:S(2)}) collective-permute-start(bf16[512,1024]{1,0:T(8,128)(2,1)S(1)} %get-tuple-element.42), channel_id=1, source_target_pairs={{0,24},{8,0},{16,8},{24,16},{1,25},{9,1},{17,9},{25,17},{2,26},{10... | collective-permute-start | bytes 3145736 | tf_op jit(solution)/shard_map/ppermute | solution.py:202
  7.8 61.9 %collective-permute-start.2 = (bf16[512,1024]{1,0:T(8,128)(2,1)}, bf16[512,1024]{1,0:T(8,128)(2,1)}, u32[]{:S(2)}, u32[]{:S(2)}) collective-permute-start(bf16[512,1024]{1,0:T(8,128)(2,1)} %get-tuple-element.43), channel_id=1, source_target_pairs={{0,24},{8,0},{16,8},{24,16},{1,25},{9,1},{17,9},{25,17},{2,26},{10... | collective-permute-start | bytes 3145736 | tf_op jit(solution)/shard_map/ppermute | solution.py:202
  7.9 47.5 %copy-start.5 = (f32[1,48]{1,0:T(1,128)}, f32[1,48]{1,0:T(1,128)S(1)}, u32[]{:S(2)}) copy-start(f32[1,48]{1,0:T(1,128)S(1)} %neg.9.rate) | copy-start | bytes 580
  8.0 47.4 %copy-start.6 = (f32[1,48]{1,0:T(1,128)}, f32[1,48]{1,0:T(1,128)S(1)}, u32[]{:S(2)}) copy-start(f32[1,48]{1,0:T(1,128)S(1)} %tile.33.bias) | copy-start | bytes 580
  8.3 47.1 %copy-start.3 = (bf16[2048,48]{1,0:T(8,128)(2,1)}, bf16[2048,48]{1,0:T(8,128)(2,1)S(1)}, u32[]{:S(2)}) copy-start(bf16[2048,48]{1,0:T(8,128)(2,1)S(1)} %copy.22.raw) | copy-start | bytes 589828
  8.4 47.0 %copy-start.4 = (bf16[48,1024]{1,0:T(8,128)(2,1)}, bf16[48,1024]{1,0:T(8,128)(2,1)S(1)}, u32[]{:S(2)}) copy-start(bf16[48,1024]{1,0:T(8,128)(2,1)S(1)} %compare_convert_fusion.1.onehot) | copy-start | bytes 294916
  10.2 2.2 %copy-start = (bf16[1,2048,1024]{2,1,0:T(8,128)(2,1)S(1)}, bf16[1,2048,1024]{2,1,0:T(8,128)(2,1)}, u32[]{:S(2)}) copy-start(bf16[1,2048,1024]{2,1,0:T(8,128)(2,1)} %param.9) | copy-start | bytes 12582916
  12.4 45.1 %copy-start.10 = (f32[1,16]{1,0:T(1,128)S(1)}, f32[1,16]{1,0:T(1,128)}, u32[]{:S(2)}) copy-start(f32[1,16]{1,0:T(1,128)} %param.15) | copy-start | bytes 196
  55.4 1.0 %copy-start.1 = (bf16[256,2048]{1,0:T(8,128)(2,1)}, bf16[256,2048]{1,0:T(8,128)(2,1)S(1)}, u32[]{:S(2)}) copy-start(bf16[256,2048]{1,0:T(8,128)(2,1)S(1)} %get-tuple-element.19.bt) | copy-start | bytes 3145732
  56.4 1.0 %copy-start.2 = (bf16[256,2048]{1,0:T(8,128)(2,1)}, bf16[256,2048]{1,0:T(8,128)(2,1)S(1)}, u32[]{:S(2)}) copy-start(bf16[256,2048]{1,0:T(8,128)(2,1)S(1)} %get-tuple-element.20.ct) | copy-start | bytes 3145732
  59.1 1.7 %copy-start.7 = (bf16[512,1024]{1,0:T(8,128)(2,1)}, bf16[512,1024]{1,0:T(8,128)(2,1)S(1)}, u32[]{:S(2)}) copy-start(bf16[512,1024]{1,0:T(8,128)(2,1)S(1)} %collective-permute-done.3.g) | copy-start | bytes 3145732

commit v3 on v2

--- a/solution.py
+++ b/solution.py
@@ -4,6 +4,7 @@
 
 import jax
 import jax.numpy as jnp
+import numpy as np
 from jax import lax
 from jax.experimental import pallas as pl
 from jax.experimental.pallas import tpu as pltpu
@@ -14,7 +15,6 @@
 G = 4
 SPAN = 256
 COPIES = 3
-CHUNKS = 4
 F32, BF16 = jnp.float32, jnp.bfloat16
 
 
@@ -68,7 +68,8 @@
     return step, slope, jnp.exp(cum - middle), jnp.exp(middle - cum), jnp.exp(middle)
 
 
-def forward_sends(blocks, per_group, raw, bias, rate, out, x, onehot, ybar, bt, ct, state, land, send1, recv1, send2, recv2):
+def forward_sends(blocks, per_group, raw, bias, rate, out, x, onehot, ct, *rest):
+    outs, (bt, state, land, send1, recv1, send2, recv2) = rest[:-7], rest[-7:]
     now = pl.program_id(0)
     me = lax.axis_index("tp")
     group, place = me // per_group, me % per_group
@@ -139,7 +140,7 @@
         beside(now, d).wait_recv()
     bt[...] = land[now, :, :, 0].reshape(N, SPAN)
     ct[...] = land[now, :, :, 1].reshape(N, SPAN)
-    forward_kernel(raw, bias, rate, bt, ct, x, onehot, ybar, state)
+    forward_kernel(raw, bias, rate, bt, ct, x, onehot, *outs, state)
 
     @pl.when(now == blocks - 1)
     def _():
@@ -151,15 +152,23 @@
                 beside(j, d).wait_send()
 
 
-def forward_kernel(raw, bias, rate, bt, ct, x, onehot, ybar, state):
+def forward_kernel(
+    raw, bias, rate, bt, ct, x, onehot, ybar, wide_rise, wide_fall, turned_hi, turned_lo, b_out, step_out, slope_out, rise_out, fall_out, state
+):
     @pl.when(pl.program_id(0) == 0)
     def _():
         state[...] = jnp.zeros_like(state)
 
-    step, _, _, fall, half = steps(raw[...], bias[...], rate[...])
+    step, slope, rise, fall, half = steps(raw[...], bias[...], rate[...])
+    step_out[...], slope_out[...], rise_out[...], fall_out[...] = step, slope, rise, fall
+    wide_rise[...] = widen(rise, onehot[...])
+    scale = widen(step * fall, onehot[...])
+    wide_fall[...] = scale
     half_row = widen(jnp.broadcast_to(half, (8, half.shape[1])), onehot[...])[0:1]
-    x_hi, x_lo = split2(x[...].astype(F32) * widen(step * fall, onehot[...]))
-    c_rows = ct[...].T
+    x_hi, x_lo = split2(x[...].astype(F32) * scale)
+    c_rows, b_rows = ct[...].T, bt[...].T
+    b_out[...] = b_rows
+    turned_hi[...], turned_lo[...] = split2(jnp.where(triangle(False), dot(b_rows, ct[...]), 0.0))
     s_hi, s_lo = split2(jnp.where(triangle(True), dot(c_rows, bt[...]), 0.0))
     held = half_row * state[...]
     t_hi, t_lo = split2(held)
@@ -168,33 +177,39 @@
 
 
 def backward_kernel(
-    raw, bias, rate, bt, ct, x, g, ybar, onehot, onehot_t, skip, state_in, carry_in, *rest
+    x, g, ybar, wide_rise, wide_fall, s_hi, s_lo, b_rows, ct, step, slope, rise, fall,
+    rate, skip, onehot, onehot_t, grad_x, grad_dt, state, by_all, decay_all
 ):
-    grad_x, grad_dt, state, carry = rest[-4:]
-
-    @pl.when(pl.program_id(0) == 0)
-    def _():
-        state[...] = state_in[...]
-        carry[...] = carry_in[...]
-
-    step, slope, rise, fall, _ = steps(raw[...], bias[...], rate[...])
-    wide_rise = widen(rise, onehot[...])
+    now, blocks = pl.program_id(0), pl.num_programs(0)
+
+    @pl.when(now == 0)
+    def _():
+        state[...] = jnp.zeros_like(state)
+
     half_row = wide_rise[SPAN - 1 :, :]
     grad = g[...].astype(F32)
-    g_hi, g_lo = split2(grad * wide_rise)
-    b_rows = bt[...].T
-    s_hi, s_lo = split2(jnp.where(triangle(False), dot(b_rows, ct[...]), 0.0))
+    g_hi, g_lo = split2(grad * wide_rise[...])
     held = half_row * state[...]
     t_hi, t_lo = split2(held)
-    zbar = dot(s_hi, g_hi) + dot(s_hi, g_lo) + dot(s_lo, g_hi) + dot(b_rows, t_hi) + dot(b_rows, t_lo)
+    zbar = dot(s_hi[...], g_hi) + dot(s_hi[...], g_lo) + dot(s_lo[...], g_hi) + dot(b_rows[...], t_hi) + dot(b_rows[...], t_lo)
     state[...] = half_row * (held + dot(ct[...], g_hi) + dot(ct[...], g_lo))
-    grad_x[...] = (widen(step * fall, onehot[...]) * zbar + skip[...] * grad).astype(BF16)
-    by_x = fall * head_sum(x[...].astype(F32) * zbar, onehot_t[...])
-    by_y = rise * head_sum(grad * ybar[...], onehot_t[...])
-    decay = running(triangle(False), by_y - step * by_x) + carry[0:1, :]
-    carry[...] = jnp.broadcast_to(decay[0:1, :], carry.shape)
-    heads = grad_dt.shape[1]
-    grad_dt[...] = (slope * (by_x + rate[...] * decay))[:, :heads].astype(BF16)
+    skip_row = widen(jnp.broadcast_to(skip[...], (8, skip.shape[1])), onehot[...])[0:1]
+    grad_x[...] = (wide_fall[...] * zbar + skip_row * grad).astype(BF16)
+    by_x = fall[...] * head_sum(x[...].astype(F32) * zbar, onehot_t[...])
+    by_y = rise[...] * head_sum(grad * ybar[...], onehot_t[...])
+    here = pl.ds(pl.multiple_of((blocks - 1 - now) * SPAN, SPAN), SPAN)
+    by_all[here, :] = by_x
+    decay_all[here, :] = by_y - step[...] * by_x
+
+    @pl.when(now == blocks - 1)
+    def _():
+        length, heads = grad_dt.shape
+        carry = jnp.zeros((1, by_all.shape[1]), F32)
+        for j in range(length // SPAN - 1, -1, -1):
+            part = slice(j * SPAN, (j + 1) * SPAN)
+            decay = running(triangle(False), decay_all[part, :]) + carry
+            carry = decay[0:1, :]
+            grad_dt[part, :] = (slope[part, :] * (by_all[part, :] + rate[...] * decay))[:, :heads].astype(BF16)
 
 
 def shifted(value, axis, by):
@@ -206,11 +221,11 @@
     length, columns = b_proj.shape
     width = columns // G
     blocks = length // SPAN
-    kind = jnp.arange(2 * columns) // width % 2
-    entry = jnp.arange(2 * columns) // (2 * width) + jnp.arange(2 * columns) % width * G
-    take = jnp.arange(columns)[None, :]
+    kind = np.arange(2 * columns) // width % 2
+    entry = np.arange(2 * columns) // (2 * width) + np.arange(2 * columns) % width * G
+    take = np.arange(columns)[None, :]
     sides = [((entry[:, None] == take) & (kind[:, None] == which)).astype(BF16) for which in range(2)]
-    pick = jnp.concatenate(sides, axis=1)
+    pick = jnp.asarray(np.concatenate(sides, axis=1))
     rows = jnp.concatenate([b_proj, c_proj], axis=1).reshape(blocks, SPAN, 2 * columns)
     turned = jnp.einsum("cd,ktd->kct", pick, rows, preferred_element_type=F32).astype(BF16)
     return turned.reshape(blocks, G, 2, width, SPAN)
@@ -240,20 +255,18 @@
     length, width = inputs.shape[1:]
     heads = a_log.shape[1]
     blocks = length // SPAN
-    chunks = min(CHUNKS, blocks)
-    per_chunk = blocks // chunks
-    rows = length // chunks
-    arriving = [shifted(grad_next[0, k * rows : (k + 1) * rows], "pipe", -1) for k in range(chunks - 1, -1, -1)]
+    g = shifted(grad_next[0], "pipe", -1)
     per_group = lax.axis_size("tp") // G
     entries = b_proj.shape[2] // G
     fused = entries % 16 == 0
     raw = jnp.tile(dt_raw[0], (1, COPIES))
     bias = jnp.tile(dt_bias, (1, COPIES))
     rate = -jnp.exp(jnp.tile(a_log, (1, COPIES)))
-    skip = jnp.repeat(skip_gain, P_SIZE, axis=1)
+    skip = jnp.tile(skip_gain, (1, COPIES))
     lanes = heads * COPIES
-    onehot = (jnp.arange(lanes)[:, None] % heads == jnp.arange(width)[None, :] // P_SIZE).astype(BF16)
-    onehot_t = (jnp.arange(lanes)[None, :] % heads == jnp.arange(width)[:, None] // P_SIZE).astype(BF16)
+    onehot = (np.arange(lanes)[:, None] % heads == np.arange(width)[None, :] // P_SIZE).astype(BF16)
+    onehot_t = np.ascontiguousarray(onehot.T)
+    onehot, onehot_t = jnp.asarray(onehot), jnp.asarray(onehot_t)
     x = inputs[0]
 
     def whole(shape):
@@ -268,8 +281,12 @@
     params = pltpu.CompilerParams(vmem_limit_bytes=56 * 1024 * 1024, dimension_semantics=("arbitrary",))
     same = lambda k: k
     cost = pl.CostEstimate(flops=18 * length * N * width, bytes_accessed=8 * length * width, transcendentals=0)
+    specs, shapes = [], []
+    for columns, kind in [(width, F32)] * 3 + [(SPAN, BF16)] * 2 + [(N, BF16)] + [(lanes, F32)] * 4:
+        specs.append(token_rows(columns, same))
+        shapes.append(jax.ShapeDtypeStruct((length, columns), kind))
     if fused:
-        ybar, bt, ct = pl.pallas_call(
+        ct, *kept = pl.pallas_call(
             functools.partial(forward_sends, blocks, per_group),
             grid=(blocks,),
             in_specs=[
@@ -280,13 +297,10 @@
                 token_rows(width, same),
                 whole((lanes, width)),
             ],
-            out_specs=[token_rows(width, same), token_cols(same), token_cols(same)],
-            out_shape=[
-                jax.ShapeDtypeStruct((length, width), F32),
-                jax.ShapeDtypeStruct((N, length), BF16),
-                jax.ShapeDtypeStruct((N, length), BF16),
-            ],
+            out_specs=[token_cols(same)] + specs,
+            out_shape=[jax.ShapeDtypeStruct((N, length), BF16)] + shapes,
             scratch_shapes=[
+                pltpu.VMEM((N, SPAN), BF16),
                 pltpu.VMEM((N, width), F32),
                 pltpu.VMEM((blocks, per_group, G, 2, entries, SPAN), BF16),
                 pltpu.SemaphoreType.DMA((blocks, G)),
@@ -295,7 +309,7 @@
                 pltpu.SemaphoreType.DMA((blocks, per_group)),
             ],
             compiler_params=pltpu.CompilerParams(
-                vmem_limit_bytes=40 * 1024 * 1024,
+                vmem_limit_bytes=48 * 1024 * 1024,
                 dimension_semantics=("arbitrary",),
                 collective_id=0,
                 has_side_effects=True,
@@ -305,7 +319,7 @@
         )(raw, bias, rate, outgoing(b_proj[0], c_proj[0]), x, onehot)
     else:
         bt, ct = gather_rows(b_proj[0], c_proj[0])
-        ybar = pl.pallas_call(
+        kept = pl.pallas_call(
             forward_kernel,
             grid=(blocks,),
             in_specs=[
@@ -317,60 +331,37 @@
                 token_rows(width, same),
                 whole((lanes, width)),
             ],
-            out_specs=token_rows(width, same),
-            out_shape=jax.ShapeDtypeStruct((length, width), F32),
+            out_specs=specs,
+            out_shape=shapes,
             scratch_shapes=[pltpu.VMEM((N, width), F32)],
             compiler_params=params,
             cost_estimate=cost,
             name="states_forward",
         )(raw, bias, rate, bt, ct, x, onehot)
-
-    state = jnp.zeros((N, width), F32)
-    carry = jnp.zeros((8, lanes), F32)
-    grads = ()
-    for index, g in enumerate(arriving):
-        base = (chunks - 1 - index) * per_chunk
-        at = lambda k, base=base: base + per_chunk - 1 - k
-        local = lambda k: per_chunk - 1 - k
-        fixed = 13
-        grad_x, grad_dt, state, carry = pl.pallas_call(
-            backward_kernel,
-            grid=(per_chunk,),
-            in_specs=[
-                token_rows(lanes, at),
-                whole((1, lanes)),
-                whole((1, lanes)),
-                token_cols(at),
-                token_cols(at),
-                token_rows(width, at),
-                token_rows(width, local),
-                token_rows(width, at),
-                whole((lanes, width)),
-                whole((width, lanes)),
-                whole((1, width)),
-                whole((N, width)),
-                whole((8, lanes)),
-            ]
-            + [pl.BlockSpec(memory_space=pl.ANY)] * len(grads),
-            out_specs=[
-                token_rows(width, at),
-                token_rows(heads, at),
-                whole((N, width)),
-                whole((8, lanes)),
-            ],
-            out_shape=[
-                jax.ShapeDtypeStruct((length, width), BF16),
-                jax.ShapeDtypeStruct((length, heads), BF16),
-                jax.ShapeDtypeStruct((N, width), F32),
-                jax.ShapeDtypeStruct((8, lanes), F32),
-            ],
-            input_output_aliases={fixed: 0, fixed + 1: 1} if grads else {},
-            compiler_params=params,
-            cost_estimate=pl.CostEstimate(flops=30 * rows * N * width, bytes_accessed=12 * rows * width, transcendentals=0),
-            name="gradients_%d" % index,
-        )(raw, bias, rate, bt, ct, x, g, ybar, onehot, onehot_t, skip, state, carry, *grads)
-        grads = (grad_x, grad_dt)
-    return grads[0][None], grads[1][None]
+    ybar, wide_rise, wide_fall, turned_hi, turned_lo, b_rows, step, slope, rise, fall = kept
+    at = lambda k: blocks - 1 - k
+    grad_x, grad_dt = pl.pallas_call(
+        backward_kernel,
+        grid=(blocks,),
+        in_specs=[token_rows(width, at)] * 5
+        + [token_rows(SPAN, at)] * 2
+        + [token_rows(N, at), token_cols(at), token_rows(lanes, at), whole((length, lanes))]
+        + [token_rows(lanes, at)] * 2
+        + [whole((1, lanes)), whole((1, lanes)), whole((lanes, width)), whole((width, lanes))],
+        out_specs=[token_rows(width, at), whole((length, heads))],
+        out_shape=[
+            jax.ShapeDtypeStruct((length, width), BF16),
+            jax.ShapeDtypeStruct((length, heads), BF16),
+        ],
+        scratch_shapes=[pltpu.VMEM((N, width), F32), pltpu.VMEM((length, lanes), F32), pltpu.VMEM((length, lanes), F32)],
+        compiler_params=params,
+        cost_estimate=pl.CostEstimate(flops=24 * length * N * width, bytes_accessed=20 * length * width, transcendentals=0),
+        name="gradients",
+    )(
+        x, g, ybar, wide_rise, wide_fall, turned_hi, turned_lo, b_rows, ct, step, slope, rise, fall,
+        rate, skip, onehot, onehot_t,
+    )
+    return grad_x[None], grad_dt[None]
 
 
 def solution(mesh):

time: 98.6 us -> 86.9 us (0.88)
  Pallas kernels: 78.7 us -> 69.1 us
  local copies, waits for them, and re-layouts: 12.9 us -> 11 us
  matrix products: 1.52 us -> 2.67 us
    pallas_call x4 -> x1, Pallas kernels: 35.7 us -> 24.2 us  [body(): pl.pallas_call(backward_kernel, grid=(blocks,), in_specs=[token_rows(widt...]
    squeeze x1 -> x0, local copies, waits for them, and re-layouts: 3.98 us -> none  [body(): grad_next[0, k * rows:(k + 1) * rows]]
    broadcast_in_dim x4 -> x0, local copies, waits for them, and re-layouts: 2.45 us -> none  [the longest x1 1.1 us: body(): state = jnp.zeros((N, width), F32)]
    pallas_call x1, Pallas kernels: 43 us -> 44.8 us  [body(): pl.pallas_call(functools.partial(forward_sends, blocks, per_group), grid=...]
    unnamed x27 -> x15, local copies, waits for them, and re-layouts: 6.04 us -> 7.73 us
    another operation x0 -> x2, local copies, waits for them, and re-layouts: none -> 1.28 us  [body(): skip = jnp.tile(skip_gain, (1, COPIES))]
    dot_general x1, matrix products: 1.52 us -> 2.67 us  [outgoing(): jnp.einsum('cd,ktd->kct', pick, rows, preferred_element_type=F32)]
    convert_element_type x2 -> x0, other arithmetic: 0.99 us -> none  [the longest x1 0.91 us: body(): (jnp.arange(lanes)[None, :] % heads == jnp.arange(width)[:, None] // P_SI...]
  transfers between devices with their start and end apart: 4 -> 1, of which waited for: 0 -> 0; matrix products, arithmetic and copies ran while one was open for 6% -> 8% of each run, Pallas kernels for 71% -> 52%
where the time goes in v3:
time: 86.9 us; the launch traced here: 86.5 us
  Pallas kernels  69.1 us (80%)
  local copies, waits for them, and re-layouts  11 us (13%)
  matrix products  2.67 us (3%)
  starting transfers between devices  2.46 us (3%)
    pallas_call x1, Pallas kernels, body(): pl.pallas_call(functools.partial(forward_sends, blocks, per_group), grid=...  44.8 us
    pallas_call x1, Pallas kernels, body(): pl.pallas_call(backward_kernel, grid=(blocks,), in_specs=[token_rows(widt...  24.2 us
    unnamed x15, local copies, waits for them, and re-layouts  7.73 us
    dot_general x1, matrix products, outgoing(): jnp.einsum('cd,ktd->kct', pick, rows, preferred_element_type=F32)  2.67 us
    ppermute x1, starting transfers between devices, shifted(): lax.ppermute(value, axis, [(i, (i + by) % length) for i in range(length)])  2.46 us
  transfers between devices with their start and end apart: 1, of which 0 were waited for; matrix products, arithmetic and copies ran while one was open for 8% of the time, Pallas kernels for 52%

profile of v3, /device:TPU:0, one launch (start us, length us, event | category | flops | bytes accessed | tf_op | source)
XLA Modules:
  0.0 86.5 jit_solution(6297362391548430904)
XLA Ops:
  0.6 2.5 %collective-permute-start = (bf16[2048,1024]{1,0:T(8,128)(2,1)}, bf16[2048,1024]{1,0:T(8,128)(2,1)}, u32[]{:S(2)}, u32[]{:S(2)}) collective-permute-start(bf16[2048,1024]{1,0:T(8,128)(2,1)} %bitcast.22), channel_id=1, source_target_pairs={{0,24},{8,0},{16,8},{24,16},{1,25},{9,1},{17,9},{25,17},{2,26},{10... | collective-permute-start | bytes 12582920 | tf_op jit(solution)/shard_map/ppermute | solution.py:217
  3.1 0.7 negate_bitcast_fusion
  3.8 0.1 neg.9.rate
  3.8 0.0 copy-start
  3.8 0.7 tile.43
  4.5 0.1 tile.44.bias
  4.6 0.7 tile.47
  5.2 0.6 tile.48.skip
  5.9 0.9 tile.40
  6.7 0.3 copy.15.raw
  7.0 2.7 %convolution_convert_fusion = bf16[8,256,256]{1,2,0:T(8,128)(2,1)} fusion(bf16[256,256,1]{1,0,2:T(8,128)(2,1)} %constant.17, bf16[8,256,128]{2,1,0:T(8,128)(2,1)} %bitcast.25, bf16[8,256,128]{2,1,0:T(8,128)(2,1)} %bitcast.26), kind=kOutput, calls=%fused_computation | convolution fusion | flops 271056896 | bytes 2228224 | tf_op jit(solution)/shard_map/cd,ktd->kct/dot_general | solution.py:230
  9.7 0.0 copy-start.1
  9.7 0.9 %copy-done.1 = bf16[48,1024]{1,0:T(8,128)(2,1)S(1)} copy-done((bf16[48,1024]{1,0:T(8,128)(2,1)S(1)}, bf16[48,1024]{1,0:T(8,128)(2,1)}, u32[]{:S(2)}) %copy-start.1) | copy-done | bytes 98328
  10.6 44.8 %exchange_forward.1 = (bf16[256,2048]{1,0:T(8,128)(2,1)S(1)}, f32[2048,1024]{1,0:T(8,128)}, f32[2048,1024]{1,0:T(8,128)}, f32[2048,1024]{1,0:T(8,128)}, bf16[204...) custom-call(bf16[2048,48]{1,0:T(8,128)(2,1)S(1)} %copy.15.raw, ...), custom_call_target="tpu_custom_call" | custom-call | flops 9663676416 | bytes 16777216 | tf_op jit(solution)/shard_map/exchange_forward/pallas_call | solution.py:289
  55.4 0.0 copy-done
  55.4 0.0 copy-start.2
  55.4 1.0 %copy-done.2 = bf16[256,2048]{1,0:T(8,128)(2,1)} copy-done((bf16[256,2048]{1,0:T(8,128)(2,1)}, bf16[256,2048]{1,0:T(8,128)(2,1)S(1)}, u32[]{:S(2)}) %copy-start.2) | copy-done | bytes 1048600
  56.4 0.0 copy-start.3
  56.4 1.0 %copy-done.3 = bf16[2048,256]{1,0:T(8,128)(2,1)} copy-done((bf16[2048,256]{1,0:T(8,128)(2,1)}, bf16[2048,256]{1,0:T(8,128)(2,1)S(1)}, u32[]{:S(2)}) %copy-start.3) | copy-done | bytes 1048600
  57.4 0.0 copy-start.4
  57.4 1.0 %copy-done.4 = bf16[2048,256]{1,0:T(8,128)(2,1)} copy-done((bf16[2048,256]{1,0:T(8,128)(2,1)}, bf16[2048,256]{1,0:T(8,128)(2,1)S(1)}, u32[]{:S(2)}) %copy-start.4) | copy-done | bytes 1048600
  58.4 0.0 copy-start.5
  58.4 1.0 %copy-done.5 = bf16[2048,256]{1,0:T(8,128)(2,1)} copy-done((bf16[2048,256]{1,0:T(8,128)(2,1)}, bf16[2048,256]{1,0:T(8,128)(2,1)S(1)}, u32[]{:S(2)}) %copy-start.5) | copy-done | bytes 1048600
  59.4 0.0 copy-start.6
  59.4 1.0 %copy-done.6 = f32[2048,48]{1,0:T(8,128)} copy-done((f32[2048,48]{1,0:T(8,128)}, f32[2048,48]{1,0:T(8,128)S(1)}, u32[]{:S(2)}) %copy-start.6) | copy-done | bytes 393240
  60.4 0.0 collective-permute-done.g
  60.4 24.2 %gradients.1 = (bf16[2048,1024]{1,0:T(8,128)(2,1)}, bf16[2048,16]{1,0:T(8,128)(2,1)}) custom-call(bf16[2048,1024]{1,0:T(8,128)(2,1)} %bitcast.24, bf16[2048,1024]{1,0:T(8,128)(2,1)} %collective-permute-done.g, f32[2048,1024]{1,0:T(8,128)} %get-tuple-element.15.ybar, f32[2048,1024]{1,0:T(8,128)} %get-tuple-element.16.wide_rise, ...), custom_call_target="tpu_custom_call" | custom-call | flops 12884901888 | bytes 41943040 | tf_op jit(solution)/shard_map/gradients/pallas_call | solution.py:343
  84.6 1.8 %copy.16 = bf16[1,2048,16]{1,2,0:T(8,128)(2,1)} copy(bf16[1,2048,16]{2,1,0:T(8,128)(2,1)} %bitcast.18) | data formatting | bytes 131072
  (1 shorter events, 0.0 us)
Async XLA Ops:
  0.6 59.8 %collective-permute-start = (bf16[2048,1024]{1,0:T(8,128)(2,1)}, bf16[2048,1024]{1,0:T(8,128)(2,1)}, u32[]{:S(2)}, u32[]{:S(2)}) collective-permute-start(bf16[2048,1024]{1,0:T(8,128)(2,1)} %bitcast.22), channel_id=1, source_target_pairs={{0,24},{8,0},{16,8},{24,16},{1,25},{9,1},{17,9},{25,17},{2,26},{10... | collective-permute-start | bytes 12582920 | tf_op jit(solution)/shard_map/ppermute | solution.py:217
  3.8 51.6 %copy-start = (f32[1,48]{1,0:T(1,128)}, f32[1,48]{1,0:T(1,128)S(1)}, u32[]{:S(2)}) copy-start(f32[1,48]{1,0:T(1,128)S(1)} %neg.9.rate) | copy-start | bytes 580
  9.7 0.9 %copy-start.1 = (bf16[48,1024]{1,0:T(8,128)(2,1)S(1)}, bf16[48,1024]{1,0:T(8,128)(2,1)}, u32[]{:S(2)}) copy-start(bf16[48,1024]{1,0:T(8,128)(2,1)} %constant.6.clone.onehot) | copy-start | bytes 294916
  55.4 1.0 %copy-start.2 = (bf16[256,2048]{1,0:T(8,128)(2,1)}, bf16[256,2048]{1,0:T(8,128)(2,1)S(1)}, u32[]{:S(2)}) copy-start(bf16[256,2048]{1,0:T(8,128)(2,1)S(1)} %get-tuple-element.21.ct) | copy-start | bytes 3145732
  56.4 1.0 %copy-start.3 = (bf16[2048,256]{1,0:T(8,128)(2,1)}, bf16[2048,256]{1,0:T(8,128)(2,1)S(1)}, u32[]{:S(2)}) copy-start(bf16[2048,256]{1,0:T(8,128)(2,1)S(1)} %get-tuple-element.18.s_hi) | copy-start | bytes 3145732
  57.4 1.0 %copy-start.4 = (bf16[2048,256]{1,0:T(8,128)(2,1)}, bf16[2048,256]{1,0:T(8,128)(2,1)S(1)}, u32[]{:S(2)}) copy-start(bf16[2048,256]{1,0:T(8,128)(2,1)S(1)} %get-tuple-element.19.s_lo) | copy-start | bytes 3145732
  58.4 1.0 %copy-start.5 = (bf16[2048,256]{1,0:T(8,128)(2,1)}, bf16[2048,256]{1,0:T(8,128)(2,1)S(1)}, u32[]{:S(2)}) copy-start(bf16[2048,256]{1,0:T(8,128)(2,1)S(1)} %get-tuple-element.20.b_rows) | copy-start | bytes 3145732
  59.4 1.0 %copy-start.6 = (f32[2048,48]{1,0:T(8,128)}, f32[2048,48]{1,0:T(8,128)S(1)}, u32[]{:S(2)}) copy-start(f32[2048,48]{1,0:T(8,128)S(1)} %get-tuple-element.22.step) | copy-start | bytes 1179652

commit v4 on v3

--- a/solution.py
+++ b/solution.py
@@ -68,7 +68,7 @@
     return step, slope, jnp.exp(cum - middle), jnp.exp(middle - cum), jnp.exp(middle)
 
 
-def forward_sends(blocks, per_group, raw, bias, rate, out, x, onehot, ct, *rest):
+def forward_sends(blocks, per_group, raw, heads_of, out, x, onehot, ct, *rest):
     outs, (bt, state, land, send1, recv1, send2, recv2) = rest[:-7], rest[-7:]
     now = pl.program_id(0)
     me = lax.axis_index("tp")
@@ -140,7 +140,7 @@
         beside(now, d).wait_recv()
     bt[...] = land[now, :, :, 0].reshape(N, SPAN)
     ct[...] = land[now, :, :, 1].reshape(N, SPAN)
-    forward_kernel(raw, bias, rate, bt, ct, x, onehot, *outs, state)
+    forward_kernel(raw, heads_of, bt, ct, x, onehot, *outs, state)
 
     @pl.when(now == blocks - 1)
     def _():
@@ -153,13 +153,13 @@
 
 
 def forward_kernel(
-    raw, bias, rate, bt, ct, x, onehot, ybar, wide_rise, wide_fall, turned_hi, turned_lo, b_out, step_out, slope_out, rise_out, fall_out, state
+    raw, heads_of, bt, ct, x, onehot, ybar, wide_rise, wide_fall, turned_hi, turned_lo, b_out, step_out, slope_out, rise_out, fall_out, state
 ):
     @pl.when(pl.program_id(0) == 0)
     def _():
         state[...] = jnp.zeros_like(state)
 
-    step, slope, rise, fall, half = steps(raw[...], bias[...], rate[...])
+    step, slope, rise, fall, half = steps(raw[...], heads_of[0:1, :], -jnp.exp(heads_of[1:2, :]))
     step_out[...], slope_out[...], rise_out[...], fall_out[...] = step, slope, rise, fall
     wide_rise[...] = widen(rise, onehot[...])
     scale = widen(step * fall, onehot[...])
@@ -178,7 +178,7 @@
 
 def backward_kernel(
     x, g, ybar, wide_rise, wide_fall, s_hi, s_lo, b_rows, ct, step, slope, rise, fall,
-    rate, skip, onehot, onehot_t, grad_x, grad_dt, state, by_all, decay_all
+    heads_of, onehot, onehot_t, grad_x, grad_dt, state, by_all, decay_all
 ):
     now, blocks = pl.program_id(0), pl.num_programs(0)
 
@@ -193,7 +193,7 @@
     t_hi, t_lo = split2(held)
     zbar = dot(s_hi[...], g_hi) + dot(s_hi[...], g_lo) + dot(s_lo[...], g_hi) + dot(b_rows[...], t_hi) + dot(b_rows[...], t_lo)
     state[...] = half_row * (held + dot(ct[...], g_hi) + dot(ct[...], g_lo))
-    skip_row = widen(jnp.broadcast_to(skip[...], (8, skip.shape[1])), onehot[...])[0:1]
+    skip_row = widen(jnp.broadcast_to(heads_of[2:3, :], (8, heads_of.shape[1])), onehot[...])[0:1]
     grad_x[...] = (wide_fall[...] * zbar + skip_row * grad).astype(BF16)
     by_x = fall[...] * head_sum(x[...].astype(F32) * zbar, onehot_t[...])
     by_y = rise[...] * head_sum(grad * ybar[...], onehot_t[...])
@@ -209,7 +209,7 @@
             part = slice(j * SPAN, (j + 1) * SPAN)
             decay = running(triangle(False), decay_all[part, :]) + carry
             carry = decay[0:1, :]
-            grad_dt[part, :] = (slope[part, :] * (by_all[part, :] + rate[...] * decay))[:, :heads].astype(BF16)
+            grad_dt[part, :] = (slope[part, :] * (by_all[part, :] - jnp.exp(heads_of[1:2, :]) * decay))[:, :heads].astype(BF16)
 
 
 def shifted(value, axis, by):
@@ -260,9 +260,7 @@
     entries = b_proj.shape[2] // G
     fused = entries % 16 == 0
     raw = jnp.tile(dt_raw[0], (1, COPIES))
-    bias = jnp.tile(dt_bias, (1, COPIES))
-    rate = -jnp.exp(jnp.tile(a_log, (1, COPIES)))
-    skip = jnp.tile(skip_gain, (1, COPIES))
+    heads_of = jnp.tile(jnp.concatenate([dt_bias, a_log, skip_gain], axis=0), (1, COPIES))
     lanes = heads * COPIES
     onehot = (np.arange(lanes)[:, None] % heads == np.arange(width)[None, :] // P_SIZE).astype(BF16)
     onehot_t = np.ascontiguousarray(onehot.T)
@@ -278,7 +276,7 @@
     def token_cols(at):
         return pl.BlockSpec((N, SPAN), lambda k: (0, at(k)))
 
-    params = pltpu.CompilerParams(vmem_limit_bytes=56 * 1024 * 1024, dimension_semantics=("arbitrary",))
+    params = pltpu.CompilerParams(vmem_limit_bytes=62 * 1024 * 1024, dimension_semantics=("arbitrary",))
     same = lambda k: k
     cost = pl.CostEstimate(flops=18 * length * N * width, bytes_accessed=8 * length * width, transcendentals=0)
     specs, shapes = [], []
@@ -291,8 +289,7 @@
             grid=(blocks,),
             in_specs=[
                 token_rows(lanes, same),
-                whole((1, lanes)),
-                whole((1, lanes)),
+                whole((3, lanes)),
                 pl.BlockSpec(memory_space=pl.ANY),
                 token_rows(width, same),
                 whole((lanes, width)),
@@ -309,14 +306,14 @@
                 pltpu.SemaphoreType.DMA((blocks, per_group)),
             ],
             compiler_params=pltpu.CompilerParams(
-                vmem_limit_bytes=48 * 1024 * 1024,
+                vmem_limit_bytes=60 * 1024 * 1024,
                 dimension_semantics=("arbitrary",),
                 collective_id=0,
                 has_side_effects=True,
             ),
             cost_estimate=cost,
             name="exchange_forward",
-        )(raw, bias, rate, outgoing(b_proj[0], c_proj[0]), x, onehot)
+        )(raw, heads_of, outgoing(b_proj[0], c_proj[0]), x, onehot)
     else:
         bt, ct = gather_rows(b_proj[0], c_proj[0])
         kept = pl.pallas_call(
@@ -324,8 +321,7 @@
             grid=(blocks,),
             in_specs=[
                 token_rows(lanes, same),
-                whole((1, lanes)),
-                whole((1, lanes)),
+                whole((3, lanes)),
                 token_cols(same),
                 token_cols(same),
                 token_rows(width, same),
@@ -337,7 +333,7 @@
             compiler_params=params,
             cost_estimate=cost,
             name="states_forward",
-        )(raw, bias, rate, bt, ct, x, onehot)
+        )(raw, heads_of, bt, ct, x, onehot)
     ybar, wide_rise, wide_fall, turned_hi, turned_lo, b_rows, step, slope, rise, fall = kept
     at = lambda k: blocks - 1 - k
     grad_x, grad_dt = pl.pallas_call(
@@ -347,7 +343,7 @@
         + [token_rows(SPAN, at)] * 2
         + [token_rows(N, at), token_cols(at), token_rows(lanes, at), whole((length, lanes))]
         + [token_rows(lanes, at)] * 2
-        + [whole((1, lanes)), whole((1, lanes)), whole((lanes, width)), whole((width, lanes))],
+        + [whole((3, lanes)), whole((lanes, width)), whole((width, lanes))],
         out_specs=[token_rows(width, at), whole((length, heads))],
         out_shape=[
             jax.ShapeDtypeStruct((length, width), BF16),
@@ -359,7 +355,7 @@
         name="gradients",
     )(
         x, g, ybar, wide_rise, wide_fall, turned_hi, turned_lo, b_rows, ct, step, slope, rise, fall,
-        rate, skip, onehot, onehot_t,
+        heads_of, onehot, onehot_t,
     )
     return grad_x[None], grad_dt[None]
 

time: 86.9 us -> 80.4 us (0.925)
  local copies, waits for them, and re-layouts: 11 us -> 4.38 us
    unnamed x15 -> x1, local copies, waits for them, and re-layouts: 7.73 us -> 1.85 us
    another operation x5 -> x2, local copies, waits for them, and re-layouts: 2.03 us -> 0.67 us  [body(): jnp.tile(jnp.concatenate([dt_bias, a_log, skip_gain], axis=0), (1, COPIES))]
  transfers between devices with their start and end apart: 1 -> 1, of which waited for: 0 -> 0; matrix products, arithmetic and copies ran while one was open for 8% -> 7% of each run, Pallas kernels for 52% -> 56%
where the time goes in v4:
time: 80.4 us; the launch traced here: 80.1 us
  Pallas kernels  69.2 us (86%)
  local copies, waits for them, and re-layouts  4.38 us (5%)
  matrix products  2.66 us (3%)
  starting transfers between devices  2.46 us (3%)
    pallas_call x1, Pallas kernels, body(): pl.pallas_call(functools.partial(forward_sends, blocks, per_group), grid=...  45.1 us
    pallas_call x1, Pallas kernels, body(): pl.pallas_call(backward_kernel, grid=(blocks,), in_specs=[token_rows(widt...  24.1 us
    dot_general x1, matrix products, outgoing(): jnp.einsum('cd,ktd->kct', pick, rows, preferred_element_type=F32)  2.66 us
    ppermute x1, starting transfers between devices, shifted(): lax.ppermute(value, axis, [(i, (i + by) % length) for i in range(length)])  2.46 us
    another operation x2, local copies, waits for them, and re-layouts, body(): raw = jnp.tile(dt_raw[0], (1, COPIES))  1.87 us
    unnamed x1, local copies, waits for them, and re-layouts  1.85 us
  transfers between devices with their start and end apart: 1, of which 0 were waited for; matrix products, arithmetic and copies ran while one was open for 7% of the time, Pallas kernels for 56%

profile of v4, /device:TPU:0, one launch (start us, length us, event | category | flops | bytes accessed | tf_op | source)
XLA Modules:
  0.0 80.1 jit_solution(7254145897769858589)
XLA Ops:
  0.6 2.5 %collective-permute-start = (bf16[2048,1024]{1,0:T(8,128)(2,1)}, bf16[2048,1024]{1,0:T(8,128)(2,1)}, u32[]{:S(2)}, u32[]{:S(2)}) collective-permute-start(bf16[2048,1024]{1,0:T(8,128)(2,1)} %bitcast.16), channel_id=1, source_target_pairs={{0,24},{8,0},{16,8},{24,16},{1,25},{9,1},{17,9},{25,17},{2,26},{10... | collective-permute-start | bytes 12582920 | tf_op jit(solution)/shard_map/ppermute | solution.py:217
  3.1 0.7 pad_maximum_fusion
  3.8 0.7 tile.23.heads_of
  4.5 0.9 %tile.20 = bf16[2048,3,16]{0,2,1:T(8,128)(2,1)S(1)} broadcast(bf16[2048,16]{0,1:T(8,128)(2,1)} %bitcast.15), dimensions={0,2} | broadcast | bytes 262144 | tf_op jit(solution)/shard_map/tile | solution.py:262
  5.3 1.0 %copy.15.raw = bf16[2048,48]{1,0:T(8,128)(2,1)} copy(bf16[2048,48]{0,1:T(8,128)(2,1)S(1)} %bitcast.13) | data formatting | bytes 393216 | tf_op jit(solution)/shard_map/tile | solution.py:262
  6.3 2.7 %convolution_convert_fusion = bf16[8,256,256]{1,2,0:T(8,128)(2,1)} fusion(bf16[256,256,1]{1,0,2:T(8,128)(2,1)} %constant.17, bf16[8,256,128]{2,1,0:T(8,128)(2,1)} %bitcast.19, bf16[8,256,128]{2,1,0:T(8,128)(2,1)} %bitcast.20), kind=kOutput, calls=%fused_computation | convolution fusion | flops 271056896 | bytes 2228224 | tf_op jit(solution)/shard_map/cd,ktd->kct/dot_general | solution.py:230
  9.0 45.1 %exchange_forward.1 = (bf16[256,2048]{1,0:T(8,128)(2,1)}, f32[2048,1024]{1,0:T(8,128)}, f32[2048,1024]{1,0:T(8,128)}, f32[2048,1024]{1,0:T(8,128)}, bf16[2048,25...) custom-call(bf16[2048,48]{1,0:T(8,128)(2,1)} %copy.15.raw, ...), custom_call_target="tpu_custom_call" | custom-call | flops 9663676416 | bytes 16777216 | tf_op jit(solution)/shard_map/exchange_forward/pallas_call | solution.py:287
  54.1 0.0 collective-permute-done.g
  54.1 24.1 %gradients.1 = (bf16[2048,1024]{1,0:T(8,128)(2,1)}, bf16[2048,16]{1,0:T(8,128)(2,1)}) custom-call(bf16[2048,1024]{1,0:T(8,128)(2,1)} %bitcast.18, bf16[2048,1024]{1,0:T(8,128)(2,1)} %collective-permute-done.g, f32[2048,1024]{1,0:T(8,128)} %get-tuple-element.15.ybar, f32[2048,1024]{1,0:T(8,128)} %get-tuple-element.16.wide_rise, ...), custom_call_target="tpu_custom_call" | custom-call | flops 12884901888 | bytes 41943040 | tf_op jit(solution)/shard_map/gradients/pallas_call | solution.py:339
  78.2 1.8 %copy.16 = bf16[1,2048,16]{1,2,0:T(8,128)(2,1)} copy(bf16[1,2048,16]{2,1,0:T(8,128)(2,1)} %bitcast.14) | data formatting | bytes 131072
  (1 shorter events, 0.0 us)
Async XLA Ops:
  0.6 53.4 %collective-permute-start = (bf16[2048,1024]{1,0:T(8,128)(2,1)}, bf16[2048,1024]{1,0:T(8,128)(2,1)}, u32[]{:S(2)}, u32[]{:S(2)}) collective-permute-start(bf16[2048,1024]{1,0:T(8,128)(2,1)} %bitcast.16), channel_id=1, source_target_pairs={{0,24},{8,0},{16,8},{24,16},{1,25},{9,1},{17,9},{25,17},{2,26},{10... | collective-permute-start | bytes 12582920 | tf_op jit(solution)/shard_map/ppermute | solution.py:217

commit v5 on v4

--- a/solution.py
+++ b/solution.py
@@ -159,7 +159,7 @@
     def _():
         state[...] = jnp.zeros_like(state)
 
-    step, slope, rise, fall, half = steps(raw[...], heads_of[0:1, :], -jnp.exp(heads_of[1:2, :]))
+    step, slope, rise, fall, half = steps(raw[...].astype(F32).T, heads_of[0:1, :], -jnp.exp(heads_of[1:2, :]))
     step_out[...], slope_out[...], rise_out[...], fall_out[...] = step, slope, rise, fall
     wide_rise[...] = widen(rise, onehot[...])
     scale = widen(step * fall, onehot[...])
@@ -203,13 +203,14 @@
 
     @pl.when(now == blocks - 1)
     def _():
-        length, heads = grad_dt.shape
+        heads, length = grad_dt.shape
         carry = jnp.zeros((1, by_all.shape[1]), F32)
         for j in range(length // SPAN - 1, -1, -1):
             part = slice(j * SPAN, (j + 1) * SPAN)
             decay = running(triangle(False), decay_all[part, :]) + carry
             carry = decay[0:1, :]
-            grad_dt[part, :] = (slope[part, :] * (by_all[part, :] - jnp.exp(heads_of[1:2, :]) * decay))[:, :heads].astype(BF16)
+            turned = (slope[part, :] * (by_all[part, :] - jnp.exp(heads_of[1:2, :]) * decay)).T
+            grad_dt[:, part] = turned[:heads].astype(BF16)
 
 
 def shifted(value, axis, by):
@@ -259,7 +260,7 @@
     per_group = lax.axis_size("tp") // G
     entries = b_proj.shape[2] // G
     fused = entries % 16 == 0
-    raw = jnp.tile(dt_raw[0], (1, COPIES))
+    raw = jnp.tile(dt_raw[0].T, (COPIES, 1))
     heads_of = jnp.tile(jnp.concatenate([dt_bias, a_log, skip_gain], axis=0), (1, COPIES))
     lanes = heads * COPIES
     onehot = (np.arange(lanes)[:, None] % heads == np.arange(width)[None, :] // P_SIZE).astype(BF16)
@@ -288,7 +289,7 @@
             functools.partial(forward_sends, blocks, per_group),
             grid=(blocks,),
             in_specs=[
-                token_rows(lanes, same),
+                pl.BlockSpec((lanes, SPAN), lambda k: (0, k)),
                 whole((3, lanes)),
                 pl.BlockSpec(memory_space=pl.ANY),
                 token_rows(width, same),
@@ -320,7 +321,7 @@
             forward_kernel,
             grid=(blocks,),
             in_specs=[
-                token_rows(lanes, same),
+                pl.BlockSpec((lanes, SPAN), lambda k: (0, k)),
                 whole((3, lanes)),
                 token_cols(same),
                 token_cols(same),
@@ -344,10 +345,10 @@
         + [token_rows(N, at), token_cols(at), token_rows(lanes, at), whole((length, lanes))]
         + [token_rows(lanes, at)] * 2
         + [whole((3, lanes)), whole((lanes, width)), whole((width, lanes))],
-        out_specs=[token_rows(width, at), whole((length, heads))],
+        out_specs=[token_rows(width, at), whole((heads, length))],
         out_shape=[
             jax.ShapeDtypeStruct((length, width), BF16),
-            jax.ShapeDtypeStruct((length, heads), BF16),
+            jax.ShapeDtypeStruct((heads, length), BF16),
         ],
         scratch_shapes=[pltpu.VMEM((N, width), F32), pltpu.VMEM((length, lanes), F32), pltpu.VMEM((length, lanes), F32)],
         compiler_params=params,
@@ -357,7 +358,7 @@
         x, g, ybar, wide_rise, wide_fall, turned_hi, turned_lo, b_rows, ct, step, slope, rise, fall,
         heads_of, onehot, onehot_t,
     )
-    return grad_x[None], grad_dt[None]
+    return grad_x[None], grad_dt.T[None]
 
 
 def solution(mesh):

time: 80.4 us -> 78.2 us (0.973)
  local copies, waits for them, and re-layouts: 4.38 us -> 2.21 us
    unnamed x1 -> x0, local copies, waits for them, and re-layouts: 1.85 us -> none
    another operation x2 -> x1, local copies, waits for them, and re-layouts: 1.87 us -> 1.54 us  [body(): raw = jnp.tile(dt_raw[0].T, (COPIES, 1))]
  transfers between devices with their start and end apart: 1 -> 1, of which waited for: 0 -> 0; matrix products, arithmetic and copies ran while one was open for 7% -> 7% of each run, Pallas kernels for 56% -> 58%
where the time goes in v5:
time: 78.2 us; the launch traced here: 77.9 us
  Pallas kernels  69.3 us (89%)
  matrix products  2.66 us (3%)
  starting transfers between devices  2.46 us (3%)
  local copies, waits for them, and re-layouts  2.21 us (3%)
    pallas_call x1, Pallas kernels, body(): pl.pallas_call(functools.partial(forward_sends, blocks, per_group), grid=...  45.3 us
    pallas_call x1, Pallas kernels, body(): pl.pallas_call(backward_kernel, grid=(blocks,), in_specs=[token_rows(widt...  24 us
    dot_general x1, matrix products, outgoing(): jnp.einsum('cd,ktd->kct', pick, rows, preferred_element_type=F32)  2.66 us
    ppermute x1, starting transfers between devices, shifted(): lax.ppermute(value, axis, [(i, (i + by) % length) for i in range(length)])  2.46 us
  transfers between devices with their start and end apart: 1, of which 0 were waited for; matrix products, arithmetic and copies ran while one was open for 7% of the time, Pallas kernels for 58%

profile of v5, /device:TPU:0, one launch (start us, length us, event | category | flops | bytes accessed | tf_op | source)
XLA Modules:
  0.0 77.9 jit_solution(14945767900625917185)
XLA Ops:
  0.6 2.5 %collective-permute-start = (bf16[2048,1024]{1,0:T(8,128)(2,1)}, bf16[2048,1024]{1,0:T(8,128)(2,1)}, u32[]{:S(2)}, u32[]{:S(2)}) collective-permute-start(bf16[2048,1024]{1,0:T(8,128)(2,1)} %bitcast.19), channel_id=1, source_target_pairs={{0,24},{8,0},{16,8},{24,16},{1,25},{9,1},{17,9},{25,17},{2,26},{10... | collective-permute-start | bytes 12582920 | tf_op jit(solution)/shard_map/ppermute | solution.py:218
  3.1 0.7 pad_maximum_fusion
  3.8 0.7 tile.21.heads_of
  4.5 2.7 %convolution_convert_fusion = bf16[8,256,256]{1,2,0:T(8,128)(2,1)} fusion(bf16[256,256,1]{1,0,2:T(8,128)(2,1)} %constant.17, bf16[8,256,128]{2,1,0:T(8,128)(2,1)} %bitcast.22, bf16[8,256,128]{2,1,0:T(8,128)(2,1)} %bitcast.23), kind=kOutput, calls=%fused_computation | convolution fusion | flops 271056896 | bytes 2228224 | tf_op jit(solution)/shard_map/cd,ktd->kct/dot_general | solution.py:231
  7.1 1.5 %tile.8 = bf16[3,16,2048]{2,1,0:T(8,128)(2,1)} broadcast(bf16[16,2048]{1,0:T(8,128)(2,1)} %bitcast.18), dimensions={1,2} | broadcast | bytes 262144 | tf_op jit(solution)/shard_map/tile | solution.py:263
  8.7 45.3 %exchange_forward.1 = (bf16[256,2048]{1,0:T(8,128)(2,1)}, f32[2048,1024]{1,0:T(8,128)}, f32[2048,1024]{1,0:T(8,128)}, f32[2048,1024]{1,0:T(8,128)}, bf16[2048,25...) custom-call(bf16[48,2048]{1,0:T(8,128)(2,1)} %bitcast.17, ...), custom_call_target="tpu_custom_call" | custom-call | flops 9663676416 | bytes 16777216 | tf_op jit(solution)/shard_map/exchange_forward/pallas_call | solution.py:288
  53.9 0.0 collective-permute-done.g
  53.9 24.0 %gradients.1 = (bf16[2048,1024]{1,0:T(8,128)(2,1)}, bf16[16,2048]{1,0:T(8,128)(2,1)}) custom-call(bf16[2048,1024]{1,0:T(8,128)(2,1)} %bitcast.21, bf16[2048,1024]{1,0:T(8,128)(2,1)} %collective-permute-done.g, f32[2048,1024]{1,0:T(8,128)} %get-tuple-element.15.ybar, f32[2048,1024]{1,0:T(8,128)} %get-tuple-element.16.wide_rise, ...), custom_call_target="tpu_custom_call" | custom-call | flops 12884901888 | bytes 41943040 | tf_op jit(solution)/shard_map/gradients/pallas_call | solution.py:340
  (1 shorter events, 0.0 us)
Async XLA Ops:
  0.6 53.3 %collective-permute-start = (bf16[2048,1024]{1,0:T(8,128)(2,1)}, bf16[2048,1024]{1,0:T(8,128)(2,1)}, u32[]{:S(2)}, u32[]{:S(2)}) collective-permute-start(bf16[2048,1024]{1,0:T(8,128)(2,1)} %bitcast.19), channel_id=1, source_target_pairs={{0,24},{8,0},{16,8},{24,16},{1,25},{9,1},{17,9},{25,17},{2,26},{10... | collective-permute-start | bytes 12582920 | tf_op jit(solution)/shard_map/ppermute | solution.py:218
